TPU v7x, 256 devices: a whole 4x4x8 slice. The times are simulated.
256 devices in a mesh: grp: 8 (over x, core), row: 8 (over y, z_lo), col: 4 (over z_hi).
Axes of the slice: x: 4, y: 4, z: 8 (z_hi: 4, z_lo: 2; z = z_hi * 2 + z_lo), core: 2. Of those that a mesh axis runs over, the one named last changes fastest.
Arguments:
- root_inverse: float32 [4096, 4096], P('row', ('grp', 'col')), as said below
- panel_middle: float32 [3072, 4096], P('row', ('grp', 'col')), may hold values from -0.3125 to 0.3125
- pivot_middle: float32 [2048, 4096], P('row', ('grp', 'col')), as said below
- panel_lower: float32 [1024, 4096], P('row', ('grp', 'col')), may hold values from -0.1875 to 0.1875
- pivot_lower: float32 [1024, 4096], P('row', ('grp', 'col')), as said below
- tiles_middle: int32 [2, 24], replicated, may hold values from 0 to 31, as said below
- tiles_lower: int32 [4, 8], replicated, may hold values from 0 to 15, as said below
Outputs:
- border_middle: float32 [3072, 4096], P('row', ('grp', 'col'))
- inverse_middle: float32 [2048, 4096], P('row', ('grp', 'col'))
- border_lower: float32 [1024, 4096], P('row', ('grp', 'col'))
- inverse_lower: float32 [1024, 4096], P('row', ('grp', 'col'))
Inputs may be any that keep to these rules, and one draw needn't show every extreme that they name: `tiles_middle`: each row lists distinct tiles of the root separator, in no particular order; row 0 holds tile 0 and row 1 holds tile 32 - 1. `tiles_lower`: row f lists distinct tiles of the separator of middle front f // 2, in no particular order; even rows hold tile 0, odd rows hold tile 16 - 1. `root_inverse`: exactly symmetric. `pivot_middle`: each front's block is exactly symmetric. `pivot_lower`: each front's block is exactly symmetric.
All inputs are finite; a program needn't handle non-finite values.
Results may differ from a plain program's by a relative error of at most 0.0001.
Values sent between devices are 32-bit elements; how exact they have to be, the bound alone decides.
No kernel may reach another device: no remote copies, remote signals or barrier semaphores. Data moves between devices by JAX's collectives and lax.ppermute only.
A program may use at most 128 MiB of HBM per device.

v0:
```python
import functools

import jax
import jax.numpy as jnp
from jax import lax
from jax.experimental import pallas as pl
from jax.experimental.pallas import tpu as pltpu
from jax.sharding import PartitionSpec as P

TILE = 128
AXES = ("grp", "row", "col")
VMEM_LIMIT = 60 * 1024 * 1024


def shifted(value, axis, step):
    size = lax.axis_size(axis)
    return lax.ppermute(value, axis, [(i, (i - step) % size) for i in range(size)])


def crossed(value, axis, mask):
    size = lax.axis_size(axis)
    return lax.ppermute(value, axis, [(i, i ^ mask) for i in range(size)])


def split3(value):
    high = value.astype(jnp.bfloat16)
    low = (value - high.astype(jnp.float32)).astype(jnp.bfloat16)
    return high, low


def left3(value):
    high, low = split3(value)
    return jnp.concatenate([high, low, high], 1)


def right3(value):
    high, low = split3(value)
    return jnp.concatenate([high, high, low], 0)


def border_kernel(parts, count, places_ref, *refs):
    sources = refs[: count + 2]
    out_own, out_other = refs[count + 2 : count + 4]
    held = refs[count + 4 : -1]
    arrived = refs[-1]
    copies = [
        pltpu.make_async_copy(source, target, arrived.at[i])
        for i, (source, target) in enumerate(zip(sources, held))
    ]
    own_ref, other_ref = held[count:]
    for copy in copies[count:] + copies[:count]:
        copy.start()
    out_own[...] = jnp.zeros_like(out_own)
    out_other[...] = jnp.zeros_like(out_other)
    for copy in copies[count:]:
        copy.wait()
    waited = set()
    for tile, (index, source, size) in enumerate(parts):
        if index not in waited:
            waited.add(index)
            copies[index].wait()
        place = places_ref[tile]

        @pl.when(place >= 0)
        def _():
            at = pl.ds(pl.multiple_of(place, TILE), TILE)
            right = right3(jnp.concatenate([own_ref[at, :], other_ref[at, :]], 1))
            left = left3(held[index][source : source + size, :])
            product = jnp.dot(left, right, preferred_element_type=jnp.float32)
            out_own[...] += product[:, :TILE]
            out_other[...] += product[:, TILE:]


def border_part(arrays, parts, height, places, own, other):
    out = jax.ShapeDtypeStruct((height, TILE), jnp.float32)
    vmem = pl.BlockSpec(memory_space=pltpu.VMEM)
    operands = tuple(arrays) + (own, other)
    return pl.pallas_call(
        functools.partial(border_kernel, parts, len(arrays)),
        out_shape=(out, out),
        in_specs=[pl.BlockSpec(memory_space=pltpu.SMEM)]
        + [pl.BlockSpec(memory_space=pl.ANY)] * len(operands),
        out_specs=(vmem, vmem),
        scratch_shapes=[pltpu.VMEM(one.shape, one.dtype) for one in operands]
        + [pltpu.SemaphoreType.DMA((len(operands),))],
        compiler_params=pltpu.CompilerParams(vmem_limit_bytes=VMEM_LIMIT),
    )(places, *operands)


def inverse_kernel(halves, band_tiles, columns, tiles_ref, spots_ref, where_ref, full_ref, *refs):
    held = refs[:-4]
    pivot_ref, border_ref, inverse_ref, chosen = refs[-4:]
    count = tiles_ref.shape[0]
    me = where_ref[0]
    for q in range(count):
        at = pl.multiple_of(tiles_ref[q] * TILE, TILE)
        high, low = split3(full_ref[pl.ds(at, TILE), :])
        chosen[q, 0] = high
        chosen[q, 1] = low
    for q in range(band_tiles):
        at = pl.multiple_of(tiles_ref[me * band_tiles + q] * TILE, TILE)
        border_ref[pl.ds(q * TILE, TILE), :] = -full_ref[pl.ds(at, TILE), :]
    inverse_ref[...] = pivot_ref[...]
    for piece, (index, slot, column) in enumerate(columns):
        spot = spots_ref[piece]
        band = spot // halves
        into = pl.ds(pl.multiple_of((spot % halves) * TILE, TILE), TILE)
        total = jnp.zeros((TILE, TILE), jnp.float32)
        for q in range(band_tiles):
            left = left3(held[index][slot, :, column + q * TILE : column + (q + 1) * TILE])
            high = chosen[band * band_tiles + q, 0]
            low = chosen[band * band_tiles + q, 1]
            right = jnp.concatenate([high, high, low], 0)
            total += jnp.dot(left, right, preferred_element_type=jnp.float32)
        inverse_ref[into, :] += total


def inverse_part(full, tiles, spots, here, held, columns, pivot, band_tiles):
    count = tiles.shape[0]
    halves = pivot.shape[0] // TILE
    vmem = pl.BlockSpec(memory_space=pltpu.VMEM)
    smem = pl.BlockSpec(memory_space=pltpu.SMEM)
    return pl.pallas_call(
        functools.partial(inverse_kernel, halves, band_tiles, columns),
        out_shape=(
            jax.ShapeDtypeStruct((band_tiles * TILE, TILE), jnp.float32),
            jax.ShapeDtypeStruct(pivot.shape, jnp.float32),
        ),
        in_specs=[smem, smem, smem, vmem] + [vmem] * len(held) + [vmem],
        out_specs=(vmem, vmem),
        scratch_shapes=[pltpu.VMEM((count, 2, TILE, TILE), jnp.bfloat16)],
        compiler_params=pltpu.CompilerParams(vmem_limit_bytes=VMEM_LIMIT),
    )(tiles, spots, here, full, *held, pivot)


def gather_rows(value):
    count = lax.axis_size("row")
    copies = jnp.broadcast_to(value[None], (count,) + value.shape)
    got = lax.all_to_all(copies, "row", 0, 0, tiled=True)
    return got.reshape(-1, value.shape[1])


def swap_pairs(fronts):
    groups, rows, cols = (lax.axis_size(a) for a in AXES)
    span = groups // fronts
    slabs = span * cols
    h = slabs // rows
    pairs = []
    for g in range(groups):
        for r in range(rows):
            for c in range(cols):
                s = (g % span) * cols + c
                to_row, to_slab = s // h, r * h + s % h
                to_group = g // span * span + to_slab // cols
                source = (g * rows + r) * cols + c
                target = (to_group * rows + to_row) * cols + to_slab % cols
                pairs.append((source, target))
    return pairs


def places_of(tiles, pool):
    match = tiles[None, :] == jnp.arange(pool, dtype=jnp.int32)[:, None]
    order = jnp.arange(1, tiles.shape[0] + 1, dtype=jnp.int32)
    return jnp.sum(jnp.where(match, order[None, :], 0), axis=1) - 1


def per_device(
    root_inverse, panel_middle, pivot_middle, panel_lower, pivot_lower, tiles_middle, tiles_lower
):
    g = lax.axis_index("grp")
    r = lax.axis_index("row")
    z = lax.axis_index("col")
    x, core = g // 2, g % 2
    xh = x % 2
    steps = jnp.arange(4, dtype=jnp.int32)
    z_order = (z + steps) % 4
    pair_order = jnp.stack([xh, 1 - xh])
    core_order = jnp.stack([core, 1 - core])
    here = r.reshape(1)

    def row_slot(row):
        return (row // 2 - r // 2) % 4 * 2 + (row + r) % 2

    packed_rows = panel_middle.shape[0] + panel_lower.shape[0]
    front = lax.dynamic_index_in_dim(tiles_middle, g // 4, 0, keepdims=False)
    x_near = jnp.stack([x, (x + 1) % 4, (x + 3) % 4, (x + 2) % 4])
    z_near = jnp.stack([z, (z + 2) % 4, (z + 1) % 4, (z + 3) % 4])
    root_tiles = (core * 4 + x_near[None, :] * 8 + z_near[:, None]).reshape(-1)
    place = places_of(front, 32)[root_tiles]
    root_places = jnp.where(place < 0, -1, row_slot(place // 3) * packed_rows + place % 3 * TILE)
    middle_spots = (
        (pair_order[None, :, None] * 2 + core_order[:, None, None]) * 4 + z_order[None, None, :]
    ).reshape(-1)
    lower = lax.dynamic_index_in_dim(tiles_lower, x, 0, keepdims=False)
    parent_tiles = (pair_order[None, :] * 8 + core * 4 + z_order[:, None]).reshape(-1)
    place = places_of(lower, 16)[parent_tiles]
    parent_places = jnp.where(place < 0, -1, row_slot(place) * packed_rows + panel_middle.shape[0])
    lower_spots = (core_order[:, None] * 4 + z_order[None, :]).reshape(-1)

    own = root_inverse
    full = own.shape[0]
    half = full // 2
    wide = panel_middle.shape[0]
    panel = jnp.concatenate([panel_middle, panel_lower], 0)
    middle = TILE // 2
    tied = lax.optimization_barrier
    with jax.named_scope("step_1"):
        z_after, z_before = shifted(own, "col", 1), shifted(own, "col", -1)
        x_after, x_before = shifted(own, "grp", 2), shifted(own, "grp", -2)
        turned = lax.ppermute(panel_middle, AXES, swap_pairs(2))
        lower_turned = lax.ppermute(panel_lower, AXES, swap_pairs(4))
        panel_other = crossed(panel, "row", 1)
        y_after, y_before = shifted(panel, "row", 2), shifted(panel, "row", -2)
    z_after, z_before, x_after, x_before = tied((z_after, z_before, x_after, x_before))
    with jax.named_scope("step_2"):
        z_top = shifted(z_after[:half], "col", 1)
        z_low = shifted(z_before[half:], "col", -1)
        up_after, up_before = shifted(z_after, "grp", 2), shifted(z_after, "grp", -2)
        down_after, down_before = shifted(z_before, "grp", 2), shifted(z_before, "grp", -2)
        other_after, other_before = shifted(panel_other, "row", 2), shifted(panel_other, "row", -2)
    z_top, z_low, x_after, turned, lower_turned, y_after, y_before = tied(
        (z_top, z_low, x_after, turned, lower_turned, y_after, y_before)
    )
    with jax.named_scope("step_3"):
        far = jnp.concatenate([z_top, z_low], 0)
        far_after, far_before = shifted(far, "grp", 2), shifted(far, "grp", -2)
        x_opposite = shifted(x_after, "grp", 2)
        columns = jnp.concatenate([turned.T, lower_turned.T], 1)
        columns_after, columns_before = shifted(columns, "col", 1), shifted(columns, "col", -1)
        y_opposite = shifted(y_after, "row", 2)
        other_opposite = shifted(other_before, "row", -2)
    (
        up_after, up_before, down_after, down_before, far_after, far_before,
        x_opposite, columns_after, columns_before, y_opposite, other_opposite,
    ) = tied(
        (
            up_after, up_before, down_after, down_before, far_after, far_before,
            x_opposite, columns_after, columns_before, y_opposite, other_opposite,
        )
    )
    with jax.named_scope("step_4"):
        up_opposite = shifted(up_after, "grp", 2)
        down_opposite = shifted(down_before, "grp", -2)
        far_opposite = shifted(far_before, "grp", -2)
        columns_top = shifted(columns_after[:middle], "col", 1)
        columns_low = shifted(columns_before[middle:], "col", -1)
        slab = jnp.concatenate(
            [panel, panel_other, y_after, other_after, y_opposite, other_opposite]
            + [y_before, other_before],
            0,
        )
        slab_other = crossed(slab, "grp", 1)
    slab_other, columns_top, columns_low, up_opposite, down_opposite, far_opposite = tied(
        (slab_other, columns_top, columns_low, up_opposite, down_opposite, far_opposite)
    )
    with jax.named_scope("panel_columns"):
        columns_opposite = jnp.concatenate([columns_top, columns_low], 0)
        columns = jnp.stack([columns, columns_after, columns_opposite, columns_before])
        columns_far = crossed(columns, "grp", 1)
        columns_pair = crossed(columns[:, :, :wide], "grp", 2)
        columns_far_pair = crossed(columns_pair, "grp", 1)
        held = (columns, columns_pair, columns_far, columns_far_pair)
    with jax.named_scope("border_middle"):
        arrays = (own, x_after, x_before, x_opposite)
        arrays += (far, far_after, far_before, far_opposite)
        arrays += (z_after, up_after, up_before, up_opposite)
        arrays += (z_before, down_after, down_before, down_opposite)
        parts = [(k, 0, full) for k in range(len(arrays))]
        mine, theirs = border_part(arrays, parts, full, root_places, slab, slab_other)
        border = gather_rows(mine + crossed(theirs, "grp", 1))
    with jax.named_scope("inverse_middle"):
        spans = [(index, slot, 0) for index in range(4) for slot in range(4)]
        border_middle, inverse_middle = inverse_part(
            border, front, middle_spots, here, held, spans, pivot_middle, 3
        )
    with jax.named_scope("parent_rows"):
        own = inverse_middle
        full = own.shape[0]
        half = full // 2
        z_after, z_before = shifted(own, "col", 1), shifted(own, "col", -1)
        pair = crossed(own, "grp", 2)
        sides = jnp.concatenate([z_after, z_before], 0)
        sides_pair = crossed(sides, "grp", 2)
        z_top = shifted(z_after[:half], "col", 1)
        z_low = shifted(z_before[half:], "col", -1)
        far = jnp.concatenate([z_top, z_low], 0)
        far_pair = crossed(far, "grp", 2)
    with jax.named_scope("border_lower"):
        arrays = (own, pair, z_after, sides_pair, far, far_pair, z_before)
        parts = [(0, 0, full), (1, 0, full), (2, 0, full), (3, 0, full)]
        parts += [(4, 0, full), (5, 0, full), (6, 0, full), (3, full, full)]
        mine, theirs = border_part(arrays, parts, full, parent_places, slab, slab_other)
        border = gather_rows(mine + crossed(theirs, "grp", 1))
    with jax.named_scope("inverse_lower"):
        spans = [(index, slot, wide) for index in range(2) for slot in range(4)]
        border_lower, inverse_lower = inverse_part(
            border, lower, lower_spots, here, (columns, columns_far), spans, pivot_lower, 1
        )
    return (border_middle, inverse_middle, border_lower, inverse_lower)


def solution(mesh):
    spec = P("row", ("grp", "col"))
    return jax.shard_map(
        per_device,
        mesh=mesh,
        in_specs=(spec, spec, spec, spec, spec, P(), P()),
        out_specs=(spec, spec, spec, spec),
        check_vma=False,
    )
```

profile of v0, /device:TPU:1, one launch (start us, length us, event | category | flops | bytes accessed | tf_op | source)
XLA Modules:
  0.0 217.3 jit_solution(130545197760603376)
XLA Ops:
  0.6 6.9 %collective-permute-start = (f32[512,128]{1,0:T(8,128)}, f32[512,128]{1,0:T(8,128)S(1)}, u32[]{:S(2)}, u32[]{:S(2)}) collective-permute-start(f32[512,128]{1,0:T(8,128)} %refs_0_.1), channel_id=1, source_target_pairs={{0,3},{1,0},{2,1},{3,2},{4,7},{5,4},{6,5},{7,6},{8,11},{9,8},{10,9... | collective-permute-start | bytes 786440 | tf_op jit(solution)/shard_map/step_1/ppermute | solution.py:17
  7.6 2.5 %collective-permute-start.2 = (f32[512,128]{1,0:T(8,128)}, f32[512,128]{1,0:T(8,128)S(1)}, u32[]{:S(2)}, u32[]{:S(2)}) collective-permute-start(f32[512,128]{1,0:T(8,128)} %refs_0_.1), channel_id=1, source_target_pairs={{0,192},{32,224},{64,0},{96,32},{128,64},{160,96},{192,128},{224,1... | collective-permute-start | bytes 786440 | tf_op jit(solution)/shard_map/step_1/ppermute | solution.py:17
  10.1 1.6 constant_dynamic-update-slice_fusion.12
  11.7 1.5 constant_dynamic-update-slice_fusion.11
  13.2 2.7 %collective-permute-start.8 = (f32[512,128]{1,0:T(8,128)}, f32[512,128]{1,0:T(8,128)S(1)}, u32[]{:S(2)}, u32[]{:S(2)}) collective-permute-start(f32[512,128]{1,0:T(8,128)} %get-tuple-element.83), channel_id=1, source_target_pairs={{0,24},{4,28},{8,0},{12,4},{16,8},{20,12},{24,16},{28,20},{1,25},{... | collective-permute-start | bytes 786440 | tf_op jit(solution)/shard_map/step_1/ppermute | solution.py:17
  15.9 1.7 copy.15
  17.6 5.5 %collective-permute-start.6 = (f32[384,128]{0,1:T(8,128)}, f32[384,128]{0,1:T(8,128)}, u32[]{:S(2)}, u32[]{:S(2)}) collective-permute-start(f32[384,128]{0,1:T(8,128)} %copy.15), channel_id=1, source_target_pairs={{0,0},{1,1},{2,4},{3,5},{4,2},{5,3},{6,6},{7,7},{8,32},{9,33},{10,... | collective-permute-start | bytes 589832 | tf_op jit(solution)/shard_map/step_1/ppermute | solution.py:210
  23.3 3.9 %collective-permute-start.20 = (f32[512,128]{1,0:T(8,128)}, f32[512,128]{1,0:T(8,128)}, u32[]{:S(2)}, u32[]{:S(2)}) collective-permute-start(f32[512,128]{1,0:T(8,128)} %get-tuple-element.83), channel_id=1, source_target_pairs={{0,4},{4,0},{8,12},{12,8},{16,20},{20,16},{24,28},{28,24},{1,5},{5... | collective-permute-start | bytes 786440 | tf_op jit(solution)/shard_map/step_1/ppermute | solution.py:22
  27.2 0.9 copy.16
  28.2 5.1 %collective-permute-start.7 = (f32[128,128]{0,1:T(8,128)S(1)}, f32[128,128]{0,1:T(8,128)S(1)}, u32[]{:S(2)}, u32[]{:S(2)}) collective-permute-start(f32[128,128]{0,1:T(8,128)S(1)} %copy.16), channel_id=1, source_target_pairs={{0,0},{1,4},{2,8},{3,12},{4,1},{5,5},{6,9},{7,13},{8,2},{9,6},{10,... | collective-permute-start | bytes 196616 | tf_op jit(solution)/shard_map/step_1/ppermute | solution.py:211
  33.3 2.0 collective-permute-done.7
  35.3 4.7 %collective-permute-start.10 = (f32[512,128]{1,0:T(8,128)S(1)}, f32[512,128]{1,0:T(8,128)S(1)}, u32[]{:S(2)}, u32[]{:S(2)}) collective-permute-start(f32[512,128]{1,0:T(8,128)S(1)} %collective-permute-done.refs_8_), channel_id=1, source_target_pairs={{0,192},{32,224},{64,0},{96,32},{128,64},{160,96},{192,128},{224,1... | collective-permute-start | bytes 786440 | tf_op jit(solution)/shard_map/step_2/ppermute | solution.py:17
  40.0 5.7 %collective-permute-start.4 = (f32[256,128]{1,0:T(8,128)S(1)}, f32[256,128]{1,0:T(8,128)S(1)}, u32[]{:S(2)}, u32[]{:S(2)}) collective-permute-start(f32[256,128]{1,0:T(8,128)S(1)} %slice.21), channel_id=1, source_target_pairs={{0,3},{1,0},{2,1},{3,2},{4,7},{5,4},{6,5},{7,6},{8,11},{9,8},{10,9... | collective-permute-start | bytes 393224 | tf_op jit(solution)/shard_map/step_2/ppermute | solution.py:17
  45.8 2.7 %collective-permute-start.12 = (f32[512,128]{1,0:T(8,128)S(1)}, f32[512,128]{1,0:T(8,128)S(1)}, u32[]{:S(2)}, u32[]{:S(2)}) collective-permute-start(f32[512,128]{1,0:T(8,128)S(1)} %collective-permute-done.1.refs_12_), channel_id=1, source_target_pairs={{0,192},{32,224},{64,0},{96,32},{128,64},{160,96},{192,128},{224,1... | collective-permute-start | bytes 786440 | tf_op jit(solution)/shard_map/step_2/ppermute | solution.py:17
  48.5 3.8 %collective-permute-done.5 = f32[256,128]{1,0:T(8,128)S(1)} collective-permute-done((f32[256,128]{1,0:T(8,128)S(1)}, f32[256,128]{1,0:T(8,128)S(1)}, u32[]{:S(2)}, u32[]{:S(2)}) %collective-permute-start.5) | collective-permute-done | bytes 131104 | tf_op jit(solution)/shard_map/step_2/ppermute | solution.py:17
  52.3 3.0 %collective-permute-start.21 = (f32[512,128]{1,0:T(8,128)}, f32[512,128]{1,0:T(8,128)S(1)}, u32[]{:S(2)}, u32[]{:S(2)}) collective-permute-start(f32[512,128]{1,0:T(8,128)} %collective-permute-done.20), channel_id=1, source_target_pairs={{0,8},{4,12},{8,16},{12,20},{16,24},{20,28},{24,0},{28,4},{1,9},{5... | collective-permute-start | bytes 786440 | tf_op jit(solution)/shard_map/step_2/ppermute | solution.py:17
  55.8 1.4 collective-permute-start.15
  57.2 1.0 fusion.14
  58.2 2.0 collective-permute-done.13.refs_14_
  60.2 3.5 %collective-permute-start.17 = (f32[128,512]{1,0:T(8,128)S(1)}, f32[128,512]{1,0:T(8,128)S(1)}, u32[]{:S(2)}, u32[]{:S(2)}) collective-permute-start(f32[128,512]{1,0:T(8,128)S(1)} %get-tuple-element.79), channel_id=1, source_target_pairs={{0,3},{1,0},{2,1},{3,2},{4,7},{5,4},{6,5},{7,6},{8,11},{9,8},{10,9... | collective-permute-start | bytes 786440 | tf_op jit(solution)/shard_map/step_3/ppermute | solution.py:17
  64.6 2.4 %collective-permute-start.22 = (f32[512,128]{1,0:T(8,128)S(1)}, f32[512,128]{1,0:T(8,128)S(1)}, u32[]{:S(2)}, u32[]{:S(2)}) collective-permute-start(f32[512,128]{1,0:T(8,128)S(1)} %collective-permute-done.21), channel_id=1, source_target_pairs={{0,8},{4,12},{8,16},{12,20},{16,24},{20,28},{24,0},{28,4},{1,9},{5... | collective-permute-start | bytes 786440 | tf_op jit(solution)/shard_map/step_3/ppermute | solution.py:17
  66.9 1.0 constant_dynamic-update-slice_fusion.10
  67.9 1.0 constant_dynamic-update-slice_fusion.9
  68.9 2.4 %collective-permute-done.16.refs_3_ = f32[512,128]{1,0:T(8,128)S(1)} collective-permute-done((f32[512,128]{1,0:T(8,128)}, f32[512,128]{1,0:T(8,128)S(1)}, u32[]{:S(2)}, u32[]{:S(2)}) %collective-permute-start.16) | collective-permute-done | bytes 262176 | tf_op jit(solution)/shard_map/step_3/ppermute | solution.py:17
  71.3 2.0 collective-permute-done.18
  73.3 1.0 constant_dynamic-update-slice_fusion.5
  74.4 5.7 %collective-permute-start.24 = (f32[4096,128]{1,0:T(8,128)S(1)}, f32[4096,128]{1,0:T(8,128)}, u32[]{:S(2)}, u32[]{:S(2)}) collective-permute-start(f32[4096,128]{1,0:T(8,128)S(1)} %constant_dynamic-update-slice_fusion.4.refs_16_.refs_7_), channel_id=1, source_target_pairs={{0,32},{32,0},{64,96},{96,64},{128,160},{160,128},{192,224},{224,1... | collective-permute-start | bytes 6291464 | tf_op jit(solution)/shard_map/step_4/ppermute | solution.py:22
  80.6 2.5 %collective-permute-start.25 = (f32[64,512]{1,0:T(8,128)S(1)}, f32[64,512]{1,0:T(8,128)S(1)}, u32[]{:S(2)}, u32[]{:S(2)}) collective-permute-start(f32[64,512]{1,0:T(8,128)S(1)} %slice.23), channel_id=1, source_target_pairs={{0,3},{1,0},{2,1},{3,2},{4,7},{5,4},{6,5},{7,6},{8,11},{9,8},{10,9... | collective-permute-start | bytes 393224 | tf_op jit(solution)/shard_map/step_4/ppermute | solution.py:17
  83.1 1.7 collective-permute-start.28
  84.8 1.5 collective-permute-start.29
  86.9 4.1 %collective-permute-done.25 = f32[64,512]{1,0:T(8,128)S(1)} collective-permute-done((f32[64,512]{1,0:T(8,128)S(1)}, f32[64,512]{1,0:T(8,128)S(1)}, u32[]{:S(2)}, u32[]{:S(2)}) %collective-permute-start.25) | collective-permute-done | bytes 131104 | tf_op jit(solution)/shard_map/step_4/ppermute | solution.py:17
  91.1 2.9 %collective-permute-start.26 = (f32[64,512]{1,0:T(8,128)S(1)}, f32[64,512]{1,0:T(8,128)S(1)}, u32[]{:S(2)}, u32[]{:S(2)}) collective-permute-start(f32[64,512]{1,0:T(8,128)S(1)} %slice.24), channel_id=1, source_target_pairs={{0,1},{1,2},{2,3},{3,0},{4,5},{5,6},{6,7},{7,4},{8,9},{9,10},{10,1... | collective-permute-start | bytes 393224 | tf_op jit(solution)/shard_map/step_4/ppermute | solution.py:17
  94.5 6.0 %collective-permute-done.26 = f32[64,512]{1,0:T(8,128)S(1)} collective-permute-done((f32[64,512]{1,0:T(8,128)S(1)}, f32[64,512]{1,0:T(8,128)S(1)}, u32[]{:S(2)}, u32[]{:S(2)}) %collective-permute-start.26) | collective-permute-done | bytes 131104 | tf_op jit(solution)/shard_map/step_4/ppermute | solution.py:17
  101.3 16.9 %border_middle.1 = (f32[512,128]{1,0:T(8,128)}, f32[512,128]{1,0:T(8,128)}) custom-call(s32[16]{0:T(128)} %compare_select_fusion.12.places_ref, f32[512,128]{1,0:T(8,128)} %refs_0_.1, f32[512,128]{1,0:T(8,128)} %copy-done.13, f32[512,128]{1,0:T(8,128)} %copy-done.14, f32[512,128]{1,0:T(8,128)} %copy-done.21, f32[512,128]{1,0:T(8,128)} %copy-done.9, ...), custom_call_target="tpu_custom_call" | custom-call | tf_op jit(solution)/shard_map/border_middle/pallas_call | solution.py:78
  118.2 1.3 collective-permute-start.30
  119.5 1.4 collective-permute-done.30
  120.9 1.0 add.345
  121.9 1.5 broadcast_in_dim.39
  123.4 3.6 %all-to-all-start = ((f32[8,512,128]{2,1,0:T(8,128)}), f32[8,512,128]{2,1,0:T(8,128)S(1)}, u32[]{:S(2)}, u32[]{:S(2)}) async-start(f32[8,512,128]{2,1,0:T(8,128)} %broadcast_in_dim.39), calls=%async_computation | async-start | bytes 4194304 | tf_op jit(solution)/shard_map/border_middle/all_to_all | solution.py:139
  127.0 1.2 pad_maximum_fusion.refs_0_
  128.2 1.0 slice.32
  129.9 0.9 collective-permute-start.32
  131.5 16.9 %collective-permute-done.31.refs_1_ = f32[4,128,384]{2,1,0:T(8,128)} collective-permute-done((f32[4,128,384]{2,1,0:T(8,128)}, f32[4,128,384]{2,1,0:T(8,128)}, u32[]{:S(2)}, u32[]{:S(2)}) %collective-permute-start.31) | collective-permute-done | bytes 786464 | tf_op jit(solution)/shard_map/panel_columns/ppermute | solution.py:22
  148.3 1.2 collective-permute-start.33
  149.8 2.0 collective-permute-done.33.refs_3_
  151.8 1.9 all-to-all-done
  153.7 1.3 copy-done.3
  155.0 4.9 %inverse_middle.1 = (f32[384,128]{1,0:T(8,128)}, f32[256,128]{1,0:T(8,128)}) custom-call(s32[24]{0:T(128)} %copy-done.27, s32[16]{0:T(128)} %add.317.spots_ref, s32[1]{0:T(128)} %bitcast.5.where_ref, f32[4096,128]{1,0:T(8,128)} %bitcast.31, f32[4,128,512]{2,1,0:T(8,128)} %copy-done.1, f32[4,128,384]{2,1,0:T(8,128)} %collective-permute-done.31.refs_1_, ...), custom_call_target="tpu_custom_call" | custom-call | tf_op jit(solution)/shard_map/inverse_middle/pallas_call | solution.py:123
  159.9 1.6 collective-permute-start.35
  163.1 5.6 %collective-permute-done.35.refs_2_ = f32[256,128]{1,0:T(8,128)S(1)} collective-permute-done((f32[256,128]{1,0:T(8,128)}, f32[256,128]{1,0:T(8,128)S(1)}, u32[]{:S(2)}, u32[]{:S(2)}) %collective-permute-start.35) | collective-permute-done | bytes 131104 | tf_op jit(solution)/shard_map/parent_rows/ppermute | solution.py:17
  168.7 2.9 %collective-permute-start.38 = (f32[128,128]{1,0:T(8,128)S(1)}, f32[128,128]{1,0:T(8,128)S(1)}, u32[]{:S(2)}, u32[]{:S(2)}) collective-permute-start(f32[128,128]{1,0:T(8,128)S(1)} %slice.33), channel_id=1, source_target_pairs={{0,3},{1,0},{2,1},{3,2},{4,7},{5,4},{6,5},{7,6},{8,11},{9,8},{10,9... | collective-permute-start | bytes 196616 | tf_op jit(solution)/shard_map/parent_rows/ppermute | solution.py:17
  171.8 1.6 collective-permute-done.38
  173.4 4.3 %collective-permute-done.39 = f32[128,128]{1,0:T(8,128)S(1)} collective-permute-done((f32[128,128]{1,0:T(8,128)S(1)}, f32[128,128]{1,0:T(8,128)S(1)}, u32[]{:S(2)}, u32[]{:S(2)}) %collective-permute-start.39) | collective-permute-done | bytes 65568 | tf_op jit(solution)/shard_map/parent_rows/ppermute | solution.py:17
  177.8 1.4 collective-permute-start.40
  179.7 2.0 collective-permute-done.40.refs_5_
  183.0 4.6 %border_lower.1 = (f32[256,128]{1,0:T(8,128)}, f32[256,128]{1,0:T(8,128)}) custom-call(s32[8]{0:T(128)} %compare_select_fusion.16.places_ref, f32[256,128]{1,0:T(8,128)} %get-tuple-element.37.refs_0_, f32[256,128]{1,0:T(8,128)} %copy-done.25, f32[256,128]{1,0:T(8,128)} %copy-done.5, f32[512,128]{1,0:T(8,128)} %copy-done.24, f32[256,128]{1,0:T(8,128)} %copy-done.12, ...), custom_call_target="tpu_custom_call" | custom-call | tf_op jit(solution)/shard_map/border_lower/pallas_call | solution.py:78
  187.7 3.5 %collective-permute-start.41 = (f32[256,128]{1,0:T(8,128)}, f32[256,128]{1,0:T(8,128)S(1)}, u32[]{:S(2)}, u32[]{:S(2)}) collective-permute-start(f32[256,128]{1,0:T(8,128)} %get-tuple-element.73), channel_id=1, source_target_pairs={{0,32},{32,0},{64,96},{96,64},{128,160},{160,128},{192,224},{224,1... | collective-permute-start | bytes 393224 | tf_op jit(solution)/shard_map/border_lower/ppermute | solution.py:22
  191.1 1.2 collective-permute-done.41
  192.3 0.9 add.365
  193.2 1.1 broadcast_in_dim.43
  194.3 3.7 %all-to-all-start.1 = ((f32[8,256,128]{2,1,0:T(8,128)}), f32[8,256,128]{2,1,0:T(8,128)S(1)}, u32[]{:S(2)}, u32[]{:S(2)}) async-start(f32[8,256,128]{2,1,0:T(8,128)} %broadcast_in_dim.43), calls=%async_computation.1 | async-start | bytes 2097152 | tf_op jit(solution)/shard_map/border_lower/all_to_all | solution.py:139
  198.8 14.5 %all-to-all-done.1 = f32[8,256,128]{2,1,0:T(8,128)S(1)} async-done(((f32[8,256,128]{2,1,0:T(8,128)}), f32[8,256,128]{2,1,0:T(8,128)S(1)}, u32[]{:S(2)}, u32[]{:S(2)}) %all-to-all-start.1) | async-done | bytes 1048608 | tf_op jit(solution)/shard_map/border_lower/all_to_all | solution.py:139
  213.2 1.0 copy-done.4
  214.2 2.9 %inverse_lower.1 = (f32[128,128]{1,0:T(8,128)}, f32[128,128]{1,0:T(8,128)}) custom-call(s32[8]{0:T(128)} %copy-done.28, s32[8]{0:T(128)} %add.350.spots_ref, s32[1]{0:T(128)} %bitcast.5.where_ref, f32[2048,128]{1,0:T(8,128)} %bitcast.32, f32[4,128,512]{2,1,0:T(8,128)} %copy-done.1, f32[4,128,512]{2,1,0:T(8,128)} %collective-permute-done.32.refs_2_.refs_1_, ...), custom_call_target="tpu_custom_call" | custom-call | tf_op jit(solution)/shard_map/inverse_lower/pallas_call | solution.py:123
  (147 shorter events, 10.0 us)
Async XLA Ops:
  0.6 149.1 %copy-start = (s32[4,8]{1,0:T(4,128)S(1)}, s32[4,8]{1,0:T(4,128)}, u32[]{:S(2)}) copy-start(s32[4,8]{1,0:T(4,128)} %param.13) | copy-start | bytes 388
  0.6 17.0 %collective-permute-start = (f32[512,128]{1,0:T(8,128)}, f32[512,128]{1,0:T(8,128)S(1)}, u32[]{:S(2)}, u32[]{:S(2)}) collective-permute-start(f32[512,128]{1,0:T(8,128)} %refs_0_.1), channel_id=1, source_target_pairs={{0,3},{1,0},{2,1},{3,2},{4,7},{5,4},{6,5},{7,6},{8,11},{9,8},{10,9... | collective-permute-start | bytes 786440 | tf_op jit(solution)/shard_map/step_1/ppermute | solution.py:17
  7.6 15.6 %collective-permute-start.1 = (f32[512,128]{1,0:T(8,128)}, f32[512,128]{1,0:T(8,128)S(1)}, u32[]{:S(2)}, u32[]{:S(2)}) collective-permute-start(f32[512,128]{1,0:T(8,128)} %refs_0_.1), channel_id=1, source_target_pairs={{0,1},{1,2},{2,3},{3,0},{4,5},{5,6},{6,7},{7,4},{8,9},{9,10},{10,1... | collective-permute-start | bytes 786440 | tf_op jit(solution)/shard_map/step_1/ppermute | solution.py:17
  7.6 15.7 %collective-permute-start.2 = (f32[512,128]{1,0:T(8,128)}, f32[512,128]{1,0:T(8,128)S(1)}, u32[]{:S(2)}, u32[]{:S(2)}) collective-permute-start(f32[512,128]{1,0:T(8,128)} %refs_0_.1), channel_id=1, source_target_pairs={{0,192},{32,224},{64,0},{96,32},{128,64},{160,96},{192,128},{224,1... | collective-permute-start | bytes 786440 | tf_op jit(solution)/shard_map/step_1/ppermute | solution.py:17
  10.1 18.1 %collective-permute-start.3 = (f32[512,128]{1,0:T(8,128)}, f32[512,128]{1,0:T(8,128)S(1)}, u32[]{:S(2)}, u32[]{:S(2)}) collective-permute-start(f32[512,128]{1,0:T(8,128)} %refs_0_.1), channel_id=1, source_target_pairs={{0,64},{32,96},{64,128},{96,160},{128,192},{160,224},{192,0},{224,... | collective-permute-start | bytes 786440 | tf_op jit(solution)/shard_map/step_1/ppermute | solution.py:17
  13.2 32.5 %collective-permute-start.8 = (f32[512,128]{1,0:T(8,128)}, f32[512,128]{1,0:T(8,128)S(1)}, u32[]{:S(2)}, u32[]{:S(2)}) collective-permute-start(f32[512,128]{1,0:T(8,128)} %get-tuple-element.83), channel_id=1, source_target_pairs={{0,24},{4,28},{8,0},{12,4},{16,8},{20,12},{24,16},{28,20},{1,25},{... | collective-permute-start | bytes 786440 | tf_op jit(solution)/shard_map/step_1/ppermute | solution.py:17
  17.6 55.7 %copy-start.7 = (f32[512,128]{1,0:T(8,128)}, f32[512,128]{1,0:T(8,128)S(1)}, u32[]{:S(2)}) copy-start(f32[512,128]{1,0:T(8,128)S(1)} %collective-permute-done.refs_8_) | copy-start | bytes 786436
  17.6 22.3 %collective-permute-start.6 = (f32[384,128]{0,1:T(8,128)}, f32[384,128]{0,1:T(8,128)}, u32[]{:S(2)}, u32[]{:S(2)}) collective-permute-start(f32[384,128]{0,1:T(8,128)} %copy.15), channel_id=1, source_target_pairs={{0,0},{1,1},{2,4},{3,5},{4,2},{5,3},{6,6},{7,7},{8,32},{9,33},{10,... | collective-permute-start | bytes 589832 | tf_op jit(solution)/shard_map/step_1/ppermute | solution.py:210
  23.2 50.2 %copy-start.8 = (f32[512,128]{1,0:T(8,128)}, f32[512,128]{1,0:T(8,128)S(1)}, u32[]{:S(2)}) copy-start(f32[512,128]{1,0:T(8,128)S(1)} %collective-permute-done.1.refs_12_) | copy-start | bytes 786436
  23.2 22.5 %collective-permute-start.9 = (f32[512,128]{1,0:T(8,128)}, f32[512,128]{1,0:T(8,128)}, u32[]{:S(2)}, u32[]{:S(2)}) collective-permute-start(f32[512,128]{1,0:T(8,128)} %get-tuple-element.83), channel_id=1, source_target_pairs={{0,8},{4,12},{8,16},{12,20},{16,24},{20,28},{24,0},{28,4},{1,9},{5... | collective-permute-start | bytes 786440 | tf_op jit(solution)/shard_map/step_1/ppermute | solution.py:17
  23.3 33.9 %copy-start.13 = (f32[512,128]{1,0:T(8,128)}, f32[512,128]{1,0:T(8,128)S(1)}, u32[]{:S(2)}) copy-start(f32[512,128]{1,0:T(8,128)S(1)} %collective-permute-done.2.refs_1_) | copy-start | bytes 786436
  23.3 22.5 %collective-permute-start.20 = (f32[512,128]{1,0:T(8,128)}, f32[512,128]{1,0:T(8,128)}, u32[]{:S(2)}, u32[]{:S(2)}) collective-permute-start(f32[512,128]{1,0:T(8,128)} %get-tuple-element.83), channel_id=1, source_target_pairs={{0,4},{4,0},{8,12},{12,8},{16,20},{20,16},{24,28},{28,24},{1,5},{5... | collective-permute-start | bytes 786440 | tf_op jit(solution)/shard_map/step_1/ppermute | solution.py:22
  28.2 32.0 %copy-start.14 = (f32[512,128]{1,0:T(8,128)}, f32[512,128]{1,0:T(8,128)S(1)}, u32[]{:S(2)}) copy-start(f32[512,128]{1,0:T(8,128)S(1)} %collective-permute-done.3.refs_2_) | copy-start | bytes 786436
  28.2 7.1 %collective-permute-start.7 = (f32[128,128]{0,1:T(8,128)S(1)}, f32[128,128]{0,1:T(8,128)S(1)}, u32[]{:S(2)}, u32[]{:S(2)}) collective-permute-start(f32[128,128]{0,1:T(8,128)S(1)} %copy.16), channel_id=1, source_target_pairs={{0,0},{1,4},{2,8},{3,12},{4,1},{5,5},{6,9},{7,13},{8,2},{9,6},{10,... | collective-permute-start | bytes 196616 | tf_op jit(solution)/shard_map/step_1/ppermute | solution.py:211
  35.3 20.0 %collective-permute-start.10 = (f32[512,128]{1,0:T(8,128)S(1)}, f32[512,128]{1,0:T(8,128)S(1)}, u32[]{:S(2)}, u32[]{:S(2)}) collective-permute-start(f32[512,128]{1,0:T(8,128)S(1)} %collective-permute-done.refs_8_), channel_id=1, source_target_pairs={{0,192},{32,224},{64,0},{96,32},{128,64},{160,96},{192,128},{224,1... | collective-permute-start | bytes 786440 | tf_op jit(solution)/shard_map/step_2/ppermute | solution.py:17
  40.0 8.5 %collective-permute-start.4 = (f32[256,128]{1,0:T(8,128)S(1)}, f32[256,128]{1,0:T(8,128)S(1)}, u32[]{:S(2)}, u32[]{:S(2)}) collective-permute-start(f32[256,128]{1,0:T(8,128)S(1)} %slice.21), channel_id=1, source_target_pairs={{0,3},{1,0},{2,1},{3,2},{4,7},{5,4},{6,5},{7,6},{8,11},{9,8},{10,9... | collective-permute-start | bytes 393224 | tf_op jit(solution)/shard_map/step_2/ppermute | solution.py:17
  45.7 18.0 %copy-start.23 = (f32[512,128]{1,0:T(8,128)}, f32[512,128]{1,0:T(8,128)S(1)}, u32[]{:S(2)}) copy-start(f32[512,128]{1,0:T(8,128)S(1)} %collective-permute-done.8) | copy-start | bytes 786436
  45.7 6.6 %collective-permute-start.5 = (f32[256,128]{1,0:T(8,128)S(1)}, f32[256,128]{1,0:T(8,128)S(1)}, u32[]{:S(2)}, u32[]{:S(2)}) collective-permute-start(f32[256,128]{1,0:T(8,128)S(1)} %slice.22), channel_id=1, source_target_pairs={{0,1},{1,2},{2,3},{3,0},{4,5},{5,6},{6,7},{7,4},{8,9},{9,10},{10,1... | collective-permute-start | bytes 393224 | tf_op jit(solution)/shard_map/step_2/ppermute | solution.py:17
  45.7 9.7 %collective-permute-start.11 = (f32[512,128]{1,0:T(8,128)S(1)}, f32[512,128]{1,0:T(8,128)S(1)}, u32[]{:S(2)}, u32[]{:S(2)}) collective-permute-start(f32[512,128]{1,0:T(8,128)S(1)} %collective-permute-done.refs_8_), channel_id=1, source_target_pairs={{0,64},{32,96},{64,128},{96,160},{128,192},{160,224},{192,0},{224,... | collective-permute-start | bytes 786440 | tf_op jit(solution)/shard_map/step_2/ppermute | solution.py:17
  45.8 9.9 %collective-permute-start.12 = (f32[512,128]{1,0:T(8,128)S(1)}, f32[512,128]{1,0:T(8,128)S(1)}, u32[]{:S(2)}, u32[]{:S(2)}) collective-permute-start(f32[512,128]{1,0:T(8,128)S(1)} %collective-permute-done.1.refs_12_), channel_id=1, source_target_pairs={{0,192},{32,224},{64,0},{96,32},{128,64},{160,96},{192,128},{224,1... | collective-permute-start | bytes 786440 | tf_op jit(solution)/shard_map/step_2/ppermute | solution.py:17
  48.5 11.7 %collective-permute-start.13 = (f32[512,128]{1,0:T(8,128)S(1)}, f32[512,128]{1,0:T(8,128)S(1)}, u32[]{:S(2)}, u32[]{:S(2)}) collective-permute-start(f32[512,128]{1,0:T(8,128)S(1)} %collective-permute-done.1.refs_12_), channel_id=1, source_target_pairs={{0,64},{32,96},{64,128},{96,160},{128,192},{160,224},{192,0},{224,... | collective-permute-start | bytes 786440 | tf_op jit(solution)/shard_map/step_2/ppermute | solution.py:17
  52.3 11.4 %collective-permute-start.21 = (f32[512,128]{1,0:T(8,128)}, f32[512,128]{1,0:T(8,128)S(1)}, u32[]{:S(2)}, u32[]{:S(2)}) collective-permute-start(f32[512,128]{1,0:T(8,128)} %collective-permute-done.20), channel_id=1, source_target_pairs={{0,8},{4,12},{8,16},{12,20},{16,24},{20,28},{24,0},{28,4},{1,9},{5... | collective-permute-start | bytes 786440 | tf_op jit(solution)/shard_map/step_2/ppermute | solution.py:17
  55.2 19.1 %copy-start.15 = (f32[512,128]{1,0:T(8,128)}, f32[512,128]{1,0:T(8,128)S(1)}, u32[]{:S(2)}) copy-start(f32[512,128]{1,0:T(8,128)S(1)} %collective-permute-done.10.refs_9_) | copy-start | bytes 786436
  55.3 8.4 %collective-permute-start.23 = (f32[512,128]{1,0:T(8,128)}, f32[512,128]{1,0:T(8,128)S(1)}, u32[]{:S(2)}, u32[]{:S(2)}) collective-permute-start(f32[512,128]{1,0:T(8,128)} %collective-permute-done.20), channel_id=1, source_target_pairs={{0,24},{4,28},{8,0},{12,4},{16,8},{20,12},{24,16},{28,20},{1,25},{... | collective-permute-start | bytes 786440 | tf_op jit(solution)/shard_map/step_2/ppermute | solution.py:17
  55.4 19.0 %copy-start.9 = (f32[512,128]{1,0:T(8,128)}, f32[512,128]{1,0:T(8,128)S(1)}, u32[]{:S(2)}) copy-start(f32[512,128]{1,0:T(8,128)S(1)} %constant_dynamic-update-slice_fusion.2.refs_4_) | copy-start | bytes 786436
  55.4 19.0 %copy-start.16 = (f32[512,128]{1,0:T(8,128)}, f32[512,128]{1,0:T(8,128)S(1)}, u32[]{:S(2)}) copy-start(f32[512,128]{1,0:T(8,128)S(1)} %collective-permute-done.11.refs_10_) | copy-start | bytes 786436
  55.4 8.4 %collective-permute-start.14 = (f32[512,128]{1,0:T(8,128)S(1)}, f32[512,128]{1,0:T(8,128)S(1)}, u32[]{:S(2)}, u32[]{:S(2)}) collective-permute-start(f32[512,128]{1,0:T(8,128)S(1)} %constant_dynamic-update-slice_fusion.2.refs_4_), channel_id=1, source_target_pairs={{0,192},{32,224},{64,0},{96,32},{128,64},{160,96},{192,128},{224,1... | collective-permute-start | bytes 786440 | tf_op jit(solution)/shard_map/step_3/ppermute | solution.py:17
  55.8 18.6 %copy-start.17 = (f32[512,128]{1,0:T(8,128)}, f32[512,128]{1,0:T(8,128)S(1)}, u32[]{:S(2)}) copy-start(f32[512,128]{1,0:T(8,128)S(1)} %collective-permute-done.12.refs_13_) | copy-start | bytes 786436
  55.8 8.8 %collective-permute-start.15 = (f32[512,128]{1,0:T(8,128)S(1)}, f32[512,128]{1,0:T(8,128)S(1)}, u32[]{:S(2)}, u32[]{:S(2)}) collective-permute-start(f32[512,128]{1,0:T(8,128)S(1)} %constant_dynamic-update-slice_fusion.2.refs_4_), channel_id=1, source_target_pairs={{0,64},{32,96},{64,128},{96,160},{128,192},{160,224},{192,0},{224,... | collective-permute-start | bytes 786440 | tf_op jit(solution)/shard_map/step_3/ppermute | solution.py:17
  58.2 22.3 %copy-start.29 = (s32[2,24]{1,0:T(2,128)S(1)}, s32[2,24]{1,0:T(2,128)}, u32[]{:S(2)}) copy-start(s32[2,24]{1,0:T(2,128)} %param.12) | copy-start | bytes 580
  60.2 19.9 %copy-start.18 = (f32[512,128]{1,0:T(8,128)}, f32[512,128]{1,0:T(8,128)S(1)}, u32[]{:S(2)}) copy-start(f32[512,128]{1,0:T(8,128)S(1)} %collective-permute-done.13.refs_14_) | copy-start | bytes 786436
  60.2 11.1 %collective-permute-start.17 = (f32[128,512]{1,0:T(8,128)S(1)}, f32[128,512]{1,0:T(8,128)S(1)}, u32[]{:S(2)}, u32[]{:S(2)}) collective-permute-start(f32[128,512]{1,0:T(8,128)S(1)} %get-tuple-element.79), channel_id=1, source_target_pairs={{0,3},{1,0},{2,1},{3,2},{4,7},{5,4},{6,5},{7,6},{8,11},{9,8},{10,9... | collective-permute-start | bytes 786440 | tf_op jit(solution)/shard_map/step_3/ppermute | solution.py:17
  63.7 9.6 %collective-permute-start.18 = (f32[128,512]{1,0:T(8,128)S(1)}, f32[128,512]{1,0:T(8,128)S(1)}, u32[]{:S(2)}, u32[]{:S(2)}) collective-permute-start(f32[128,512]{1,0:T(8,128)S(1)} %get-tuple-element.79), channel_id=1, source_target_pairs={{0,1},{1,2},{2,3},{3,0},{4,5},{5,6},{6,7},{7,4},{8,9},{9,10},{10,1... | collective-permute-start | bytes 786440 | tf_op jit(solution)/shard_map/step_3/ppermute | solution.py:17
  63.7 7.6 %collective-permute-start.16 = (f32[512,128]{1,0:T(8,128)}, f32[512,128]{1,0:T(8,128)S(1)}, u32[]{:S(2)}, u32[]{:S(2)}) collective-permute-start(f32[512,128]{1,0:T(8,128)} %copy-done.13), channel_id=1, source_target_pairs={{0,192},{32,224},{64,0},{96,32},{128,64},{160,96},{192,128},{224,1... | collective-permute-start | bytes 786440 | tf_op jit(solution)/shard_map/step_3/ppermute | solution.py:17
  63.8 16.3 %copy-start.19 = (f32[512,128]{1,0:T(8,128)}, f32[512,128]{1,0:T(8,128)S(1)}, u32[]{:S(2)}) copy-start(f32[512,128]{1,0:T(8,128)S(1)} %collective-permute-done.14.refs_5_) | copy-start | bytes 786436
  63.8 9.5 %collective-permute-start.19 = (f32[512,128]{1,0:T(8,128)}, f32[512,128]{1,0:T(8,128)S(1)}, u32[]{:S(2)}, u32[]{:S(2)}) collective-permute-start(f32[512,128]{1,0:T(8,128)} %copy-done.23), channel_id=1, source_target_pairs={{0,24},{4,28},{8,0},{12,4},{16,8},{20,12},{24,16},{28,20},{1,25},{... | collective-permute-start | bytes 786440 | tf_op jit(solution)/shard_map/step_3/ppermute | solution.py:17
  64.6 15.5 %copy-start.20 = (f32[512,128]{1,0:T(8,128)}, f32[512,128]{1,0:T(8,128)S(1)}, u32[]{:S(2)}) copy-start(f32[512,128]{1,0:T(8,128)S(1)} %collective-permute-done.15.refs_6_) | copy-start | bytes 786436
  64.6 8.7 %collective-permute-start.22 = (f32[512,128]{1,0:T(8,128)S(1)}, f32[512,128]{1,0:T(8,128)S(1)}, u32[]{:S(2)}, u32[]{:S(2)}) collective-permute-start(f32[512,128]{1,0:T(8,128)S(1)} %collective-permute-done.21), channel_id=1, source_target_pairs={{0,8},{4,12},{8,16},{12,20},{16,24},{20,28},{24,0},{28,4},{1,9},{5... | collective-permute-start | bytes 786440 | tf_op jit(solution)/shard_map/step_3/ppermute | solution.py:17
  71.3 46.9 %copy-start.10 = (f32[128,512]{1,0:T(8,128)}, f32[128,512]{1,0:T(8,128)S(1)}, u32[]{:S(2)}) copy-start(f32[128,512]{1,0:T(8,128)S(1)} %collective-permute-done.17) | copy-start | bytes 786436
  73.3 48.6 %copy-start.11 = (f32[128,512]{1,0:T(8,128)}, f32[128,512]{1,0:T(8,128)S(1)}, u32[]{:S(2)}) copy-start(f32[128,512]{1,0:T(8,128)S(1)} %collective-permute-done.18) | copy-start | bytes 786436
  74.4 26.2 %copy-start.2 = (f32[4096,128]{1,0:T(8,128)}, f32[4096,128]{1,0:T(8,128)S(1)}, u32[]{:S(2)}) copy-start(f32[4096,128]{1,0:T(8,128)S(1)} %constant_dynamic-update-slice_fusion.4.refs_16_.refs_7_) | copy-start | bytes 6291460
  74.4 26.1 %collective-permute-start.24 = (f32[4096,128]{1,0:T(8,128)S(1)}, f32[4096,128]{1,0:T(8,128)}, u32[]{:S(2)}, u32[]{:S(2)}) collective-permute-start(f32[4096,128]{1,0:T(8,128)S(1)} %constant_dynamic-update-slice_fusion.4.refs_16_.refs_7_), channel_id=1, source_target_pairs={{0,32},{32,0},{64,96},{96,64},{128,160},{160,128},{192,224},{224,1... | collective-permute-start | bytes 6291464 | tf_op jit(solution)/shard_map/step_4/ppermute | solution.py:22
  80.5 37.8 %copy-start.27 = (s32[24]{0:T(128)}, s32[24]{0:T(128)S(1)}, u32[]{:S(2)}) copy-start(s32[24]{0:T(128)S(1)} %dynamic-slice_bitcast_fusion.1.tiles_ref) | copy-start | bytes 292
  80.6 10.5 %collective-permute-start.25 = (f32[64,512]{1,0:T(8,128)S(1)}, f32[64,512]{1,0:T(8,128)S(1)}, u32[]{:S(2)}, u32[]{:S(2)}) collective-permute-start(f32[64,512]{1,0:T(8,128)S(1)} %slice.23), channel_id=1, source_target_pairs={{0,3},{1,0},{2,1},{3,2},{4,7},{5,4},{6,5},{7,6},{8,11},{9,8},{10,9... | collective-permute-start | bytes 393224 | tf_op jit(solution)/shard_map/step_4/ppermute | solution.py:17
  83.1 17.4 %collective-permute-start.27 = (f32[512,128]{1,0:T(8,128)}, f32[512,128]{1,0:T(8,128)S(1)}, u32[]{:S(2)}, u32[]{:S(2)}) collective-permute-start(f32[512,128]{1,0:T(8,128)} %copy-done.15), channel_id=1, source_target_pairs={{0,192},{32,224},{64,0},{96,32},{128,64},{160,96},{192,128},{224,1... | collective-permute-start | bytes 786440 | tf_op jit(solution)/shard_map/step_4/ppermute | solution.py:17
  83.1 17.4 %collective-permute-start.28 = (f32[512,128]{1,0:T(8,128)}, f32[512,128]{1,0:T(8,128)}, u32[]{:S(2)}, u32[]{:S(2)}) collective-permute-start(f32[512,128]{1,0:T(8,128)} %copy-done.18), channel_id=1, source_target_pairs={{0,64},{32,96},{64,128},{96,160},{128,192},{160,224},{192,0},{224,... | collective-permute-start | bytes 786440 | tf_op jit(solution)/shard_map/step_4/ppermute | solution.py:17
  84.8 15.8 %collective-permute-start.29 = (f32[512,128]{1,0:T(8,128)}, f32[512,128]{1,0:T(8,128)}, u32[]{:S(2)}, u32[]{:S(2)}) collective-permute-start(f32[512,128]{1,0:T(8,128)} %copy-done.20), channel_id=1, source_target_pairs={{0,64},{32,96},{64,128},{96,160},{128,192},{160,224},{192,0},{224,... | collective-permute-start | bytes 786440 | tf_op jit(solution)/shard_map/step_4/ppermute | solution.py:17
  91.1 9.4 %collective-permute-start.26 = (f32[64,512]{1,0:T(8,128)S(1)}, f32[64,512]{1,0:T(8,128)S(1)}, u32[]{:S(2)}, u32[]{:S(2)}) collective-permute-start(f32[64,512]{1,0:T(8,128)S(1)} %slice.24), channel_id=1, source_target_pairs={{0,1},{1,2},{2,3},{3,0},{4,5},{5,6},{6,7},{7,4},{8,9},{9,10},{10,1... | collective-permute-start | bytes 393224 | tf_op jit(solution)/shard_map/step_4/ppermute | solution.py:17
  118.2 2.7 %collective-permute-start.30 = (f32[512,128]{1,0:T(8,128)}, f32[512,128]{1,0:T(8,128)S(1)}, u32[]{:S(2)}, u32[]{:S(2)}) collective-permute-start(f32[512,128]{1,0:T(8,128)} %get-tuple-element.67), channel_id=1, source_target_pairs={{0,32},{32,0},{64,96},{96,64},{128,160},{160,128},{192,224},{224,1... | collective-permute-start | bytes 786440 | tf_op jit(solution)/shard_map/border_middle/ppermute | solution.py:22
  123.4 30.3 %all-to-all-start = ((f32[8,512,128]{2,1,0:T(8,128)}), f32[8,512,128]{2,1,0:T(8,128)S(1)}, u32[]{:S(2)}, u32[]{:S(2)}) async-start(f32[8,512,128]{2,1,0:T(8,128)} %broadcast_in_dim.39), calls=%async_computation | async-start | bytes 4194304 | tf_op jit(solution)/shard_map/border_middle/all_to_all | solution.py:139
  128.2 25.4 %copy-start.1 = (f32[4,128,512]{2,1,0:T(8,128)}, f32[4,128,512]{2,1,0:T(8,128)S(1)}, u32[]{:S(2)}) copy-start(f32[4,128,512]{2,1,0:T(8,128)S(1)} %pad_maximum_fusion.refs_0_) | copy-start | bytes 3145732
  129.3 19.1 %collective-permute-start.31 = (f32[4,128,384]{2,1,0:T(8,128)}, f32[4,128,384]{2,1,0:T(8,128)}, u32[]{:S(2)}, u32[]{:S(2)}) collective-permute-start(f32[4,128,384]{2,1,0:T(8,128)} %slice.32), channel_id=1, source_target_pairs={{0,64},{32,96},{64,0},{96,32},{128,192},{160,224},{192,128},{224,1... | collective-permute-start | bytes 2359304 | tf_op jit(solution)/shard_map/panel_columns/ppermute | solution.py:22
  129.9 20.0 %collective-permute-start.32 = (f32[4,128,512]{2,1,0:T(8,128)S(1)}, f32[4,128,512]{2,1,0:T(8,128)}, u32[]{:S(2)}, u32[]{:S(2)}) collective-permute-start(f32[4,128,512]{2,1,0:T(8,128)S(1)} %pad_maximum_fusion.refs_0_), channel_id=1, source_target_pairs={{0,32},{32,0},{64,96},{96,64},{128,160},{160,128},{192,224},{224,1... | collective-permute-start | bytes 3145736 | tf_op jit(solution)/shard_map/panel_columns/ppermute | solution.py:22
  148.3 3.5 %collective-permute-start.33 = (f32[4,128,384]{2,1,0:T(8,128)}, f32[4,128,384]{2,1,0:T(8,128)}, u32[]{:S(2)}, u32[]{:S(2)}) collective-permute-start(f32[4,128,384]{2,1,0:T(8,128)} %collective-permute-done.31.refs_1_), channel_id=1, source_target_pairs={{0,32},{32,0},{64,96},{96,64},{128,160},{160,128},{192,224},{224,1... | collective-permute-start | bytes 2359304 | tf_op jit(solution)/shard_map/panel_columns/ppermute | solution.py:22
  159.9 8.8 %collective-permute-start.35 = (f32[256,128]{1,0:T(8,128)}, f32[256,128]{1,0:T(8,128)S(1)}, u32[]{:S(2)}, u32[]{:S(2)}) collective-permute-start(f32[256,128]{1,0:T(8,128)} %get-tuple-element.37.refs_0_), channel_id=1, source_target_pairs={{0,3},{1,0},{2,1},{3,2},{4,7},{5,4},{6,5},{7,6},{8,11},{9,8},{10,9... | collective-permute-start | bytes 393224 | tf_op jit(solution)/shard_map/parent_rows/ppermute | solution.py:17
  161.5 10.1 %collective-permute-start.36 = (f32[256,128]{1,0:T(8,128)}, f32[256,128]{1,0:T(8,128)S(1)}, u32[]{:S(2)}, u32[]{:S(2)}) collective-permute-start(f32[256,128]{1,0:T(8,128)} %get-tuple-element.37.refs_0_), channel_id=1, source_target_pairs={{0,1},{1,2},{2,3},{3,0},{4,5},{5,6},{6,7},{7,4},{8,9},{9,10},{10,1... | collective-permute-start | bytes 393224 | tf_op jit(solution)/shard_map/parent_rows/ppermute | solution.py:17
  162.9 16.7 %collective-permute-start.34 = (f32[256,128]{1,0:T(8,128)}, f32[256,128]{1,0:T(8,128)S(1)}, u32[]{:S(2)}, u32[]{:S(2)}) collective-permute-start(f32[256,128]{1,0:T(8,128)} %get-tuple-element.37.refs_0_), channel_id=1, source_target_pairs={{0,64},{32,96},{64,0},{96,32},{128,192},{160,224},{192,128},{224,1... | collective-permute-start | bytes 393224 | tf_op jit(solution)/shard_map/parent_rows/ppermute | solution.py:22
  168.7 13.0 %copy-start.5 = (f32[256,128]{1,0:T(8,128)}, f32[256,128]{1,0:T(8,128)S(1)}, u32[]{:S(2)}) copy-start(f32[256,128]{1,0:T(8,128)S(1)} %collective-permute-done.35.refs_2_) | copy-start | bytes 393220
  168.7 4.7 %collective-permute-start.38 = (f32[128,128]{1,0:T(8,128)S(1)}, f32[128,128]{1,0:T(8,128)S(1)}, u32[]{:S(2)}, u32[]{:S(2)}) collective-permute-start(f32[128,128]{1,0:T(8,128)S(1)} %slice.33), channel_id=1, source_target_pairs={{0,3},{1,0},{2,1},{3,2},{4,7},{5,4},{6,5},{7,6},{8,11},{9,8},{10,9... | collective-permute-start | bytes 196616 | tf_op jit(solution)/shard_map/parent_rows/ppermute | solution.py:17
  171.6 10.1 %collective-permute-start.37 = (f32[512,128]{1,0:T(8,128)S(1)}, f32[512,128]{1,0:T(8,128)S(1)}, u32[]{:S(2)}, u32[]{:S(2)}) collective-permute-start(f32[512,128]{1,0:T(8,128)S(1)} %pad_maximum_fusion.2), channel_id=1, source_target_pairs={{0,64},{32,96},{64,0},{96,32},{128,192},{160,224},{192,128},{224,1... | collective-permute-start | bytes 786440 | tf_op jit(solution)/shard_map/parent_rows/ppermute | solution.py:22
  171.8 5.9 %collective-permute-start.39 = (f32[128,128]{1,0:T(8,128)S(1)}, f32[128,128]{1,0:T(8,128)S(1)}, u32[]{:S(2)}, u32[]{:S(2)}) collective-permute-start(f32[128,128]{1,0:T(8,128)S(1)} %slice.34), channel_id=1, source_target_pairs={{0,1},{1,2},{2,3},{3,0},{4,5},{5,6},{6,7},{7,4},{8,9},{9,10},{10,1... | collective-permute-start | bytes 196616 | tf_op jit(solution)/shard_map/parent_rows/ppermute | solution.py:17
  177.8 3.9 %collective-permute-start.40 = (f32[256,128]{1,0:T(8,128)S(1)}, f32[256,128]{1,0:T(8,128)S(1)}, u32[]{:S(2)}, u32[]{:S(2)}) collective-permute-start(f32[256,128]{1,0:T(8,128)S(1)} %constant_dynamic-update-slice_fusion.13.refs_4_), channel_id=1, source_target_pairs={{0,64},{32,96},{64,0},{96,32},{128,192},{160,224},{192,128},{224,1... | collective-permute-start | bytes 393224 | tf_op jit(solution)/shard_map/parent_rows/ppermute | solution.py:22
  187.7 4.7 %collective-permute-start.41 = (f32[256,128]{1,0:T(8,128)}, f32[256,128]{1,0:T(8,128)S(1)}, u32[]{:S(2)}, u32[]{:S(2)}) collective-permute-start(f32[256,128]{1,0:T(8,128)} %get-tuple-element.73), channel_id=1, source_target_pairs={{0,32},{32,0},{64,96},{96,64},{128,160},{160,128},{192,224},{224,1... | collective-permute-start | bytes 393224 | tf_op jit(solution)/shard_map/border_lower/ppermute | solution.py:22
  194.3 18.9 %all-to-all-start.1 = ((f32[8,256,128]{2,1,0:T(8,128)}), f32[8,256,128]{2,1,0:T(8,128)S(1)}, u32[]{:S(2)}, u32[]{:S(2)}) async-start(f32[8,256,128]{2,1,0:T(8,128)} %broadcast_in_dim.43), calls=%async_computation.1 | async-start | bytes 2097152 | tf_op jit(solution)/shard_map/border_lower/all_to_all | solution.py:139
  (10 other events, 39.5 us)
where the time goes:
time: 222 us; the launch traced here: 217 us
  starting transfers between devices  87.2 us (39%)
  waiting for transfers between devices  73.6 us (33%)
  Pallas kernels  29.4 us (13%)
  local copies, waits for them, and re-layouts  19.6 us (9%)
  other arithmetic  6.01 us (3%)
    ppermute x30, starting transfers between devices, shifted(): lax.ppermute(value, axis, [(i, (i - step) % size) for i in range(size)])  50.7 us
    ppermute x30, waiting for transfers between devices, shifted(): lax.ppermute(value, axis, [(i, (i - step) % size) for i in range(size)])  31.8 us
    ppermute x10, waiting for transfers between devices, crossed(): return lax.ppermute(value, axis, [(i, i ^ mask) for i in range(size)])  23.4 us
    pallas_call x2, Pallas kernels, border_part(): pl.pallas_call(functools.partial(border_kernel, parts, len(arrays)), out_...  21.6 us
    ppermute x10, starting transfers between devices, crossed(): return lax.ppermute(value, axis, [(i, i ^ mask) for i in range(size)])  18.6 us
    all_to_all x2, waiting for transfers between devices, gather_rows(): got = lax.all_to_all(copies, 'row', 0, 0, tiled=True)  16.3 us
    unnamed x72, local copies, waits for them, and re-layouts  13.2 us
    pallas_call x2, Pallas kernels, inverse_part(): pl.pallas_call(functools.partial(inverse_kernel, halves, band_tiles, colu...  7.83 us
  transfers between devices with their start and end apart: 44, of which 17 were waited for; matrix products, arithmetic and copies ran while one was open for 7% of the time, Pallas kernels for 0%

commit v1 on v0

--- a/solution.py
+++ b/solution.py
@@ -39,32 +39,44 @@
 
 
 def border_kernel(parts, count, places_ref, *refs):
-    sources = refs[: count + 2]
+    sources = refs[:count]
+    panels = refs[count : count + 2]
     out_own, out_other = refs[count + 2 : count + 4]
-    held = refs[count + 4 : -1]
-    arrived = refs[-1]
+    held = refs[count + 4 : -3]
+    tiles, arrived, ready = refs[-3:]
     copies = [
         pltpu.make_async_copy(source, target, arrived.at[i])
         for i, (source, target) in enumerate(zip(sources, held))
     ]
-    own_ref, other_ref = held[count:]
-    for copy in copies[count:] + copies[:count]:
-        copy.start()
+    fetches = []
+    for tile in range(len(parts)):
+        at = pl.ds(pl.multiple_of(jnp.maximum(places_ref[tile], 0), TILE), TILE)
+        fetches.append(
+            [
+                pltpu.make_async_copy(panel.at[at, :], tiles.at[tile, side], ready.at[tile, side])
+                for side, panel in enumerate(panels)
+            ]
+        )
+    started = set()
+    for tile, (index, source, size) in enumerate(parts):
+        for fetch in fetches[tile]:
+            fetch.start()
+        if index not in started:
+            started.add(index)
+            copies[index].start()
     out_own[...] = jnp.zeros_like(out_own)
     out_other[...] = jnp.zeros_like(out_other)
-    for copy in copies[count:]:
-        copy.wait()
     waited = set()
     for tile, (index, source, size) in enumerate(parts):
         if index not in waited:
             waited.add(index)
             copies[index].wait()
-        place = places_ref[tile]
-
-        @pl.when(place >= 0)
+        for fetch in fetches[tile]:
+            fetch.wait()
+
+        @pl.when(places_ref[tile] >= 0)
         def _():
-            at = pl.ds(pl.multiple_of(place, TILE), TILE)
-            right = right3(jnp.concatenate([own_ref[at, :], other_ref[at, :]], 1))
+            right = right3(jnp.concatenate([tiles[tile, 0], tiles[tile, 1]], 1))
             left = left3(held[index][source : source + size, :])
             product = jnp.dot(left, right, preferred_element_type=jnp.float32)
             out_own[...] += product[:, :TILE]
@@ -81,9 +93,18 @@
         in_specs=[pl.BlockSpec(memory_space=pltpu.SMEM)]
         + [pl.BlockSpec(memory_space=pl.ANY)] * len(operands),
         out_specs=(vmem, vmem),
-        scratch_shapes=[pltpu.VMEM(one.shape, one.dtype) for one in operands]
-        + [pltpu.SemaphoreType.DMA((len(operands),))],
+        scratch_shapes=[pltpu.VMEM(one.shape, one.dtype) for one in arrays]
+        + [
+            pltpu.VMEM((len(parts), 2, TILE, TILE), jnp.float32),
+            pltpu.SemaphoreType.DMA((len(arrays),)),
+            pltpu.SemaphoreType.DMA((len(parts), 2)),
+        ],
         compiler_params=pltpu.CompilerParams(vmem_limit_bytes=VMEM_LIMIT),
+        cost_estimate=pl.CostEstimate(
+            flops=12 * len(parts) * height * TILE * TILE,
+            bytes_accessed=32 * len(parts) * height * TILE,
+            transcendentals=0,
+        ),
     )(places, *operands)
 
 
@@ -179,7 +200,7 @@
     here = r.reshape(1)
 
     def row_slot(row):
-        return (row // 2 - r // 2) % 4 * 2 + (row + r) % 2
+        return row // 2 * 2 + (row + r) % 2
 
     packed_rows = panel_middle.shape[0] + panel_lower.shape[0]
     front = lax.dynamic_index_in_dim(tiles_middle, g // 4, 0, keepdims=False)
@@ -197,6 +218,7 @@
     parent_places = jnp.where(place < 0, -1, row_slot(place) * packed_rows + panel_middle.shape[0])
     lower_spots = (core_order[:, None] * 4 + z_order[None, :]).reshape(-1)
 
+    same_z = [[0, 2, 4, 6], [1, 3, 5, 7]]
     own = root_inverse
     full = own.shape[0]
     half = full // 2
@@ -207,59 +229,52 @@
     with jax.named_scope("step_1"):
         z_after, z_before = shifted(own, "col", 1), shifted(own, "col", -1)
         x_after, x_before = shifted(own, "grp", 2), shifted(own, "grp", -2)
-        turned = lax.ppermute(panel_middle, AXES, swap_pairs(2))
-        lower_turned = lax.ppermute(panel_lower, AXES, swap_pairs(4))
         panel_other = crossed(panel, "row", 1)
-        y_after, y_before = shifted(panel, "row", 2), shifted(panel, "row", -2)
-    z_after, z_before, x_after, x_before = tied((z_after, z_before, x_after, x_before))
+        panel_pair = jnp.concatenate([panel, panel_other], 0)
+        copies = jnp.broadcast_to(panel_pair[None], (4,) + panel_pair.shape)
+    z_after, z_before, x_after, x_before, copies = tied(
+        (z_after, z_before, x_after, x_before, copies)
+    )
     with jax.named_scope("step_2"):
+        slab = lax.all_to_all(copies, "row", 0, 0, tiled=True, axis_index_groups=same_z)
+        slab = slab.reshape(-1, TILE)
         z_top = shifted(z_after[:half], "col", 1)
         z_low = shifted(z_before[half:], "col", -1)
         up_after, up_before = shifted(z_after, "grp", 2), shifted(z_after, "grp", -2)
         down_after, down_before = shifted(z_before, "grp", 2), shifted(z_before, "grp", -2)
-        other_after, other_before = shifted(panel_other, "row", 2), shifted(panel_other, "row", -2)
-    z_top, z_low, x_after, turned, lower_turned, y_after, y_before = tied(
-        (z_top, z_low, x_after, turned, lower_turned, y_after, y_before)
-    )
+    z_top, z_low, x_after = tied((z_top, z_low, x_after))
     with jax.named_scope("step_3"):
         far = jnp.concatenate([z_top, z_low], 0)
         far_after, far_before = shifted(far, "grp", 2), shifted(far, "grp", -2)
+        far_opposite = shifted(far, "grp", 4)
         x_opposite = shifted(x_after, "grp", 2)
-        columns = jnp.concatenate([turned.T, lower_turned.T], 1)
-        columns_after, columns_before = shifted(columns, "col", 1), shifted(columns, "col", -1)
-        y_opposite = shifted(y_after, "row", 2)
-        other_opposite = shifted(other_before, "row", -2)
+        up_after, up_before, down_after, down_before, panel_middle, panel_lower = tied(
+            (up_after, up_before, down_after, down_before, panel_middle, panel_lower)
+        )
+        turned = lax.ppermute(panel_middle, AXES, swap_pairs(2))
+        lower_turned = lax.ppermute(panel_lower, AXES, swap_pairs(4))
     (
-        up_after, up_before, down_after, down_before, far_after, far_before,
-        x_opposite, columns_after, columns_before, y_opposite, other_opposite,
+        up_after, down_before, far_after, far_before, far_opposite, x_opposite,
+        slab, turned, lower_turned,
     ) = tied(
         (
-            up_after, up_before, down_after, down_before, far_after, far_before,
-            x_opposite, columns_after, columns_before, y_opposite, other_opposite,
+            up_after, down_before, far_after, far_before, far_opposite, x_opposite,
+            slab, turned, lower_turned,
         )
     )
     with jax.named_scope("step_4"):
         up_opposite = shifted(up_after, "grp", 2)
         down_opposite = shifted(down_before, "grp", -2)
-        far_opposite = shifted(far_before, "grp", -2)
+        slab_other = crossed(slab, "grp", 1)
+        columns = turned.T
+        columns_after, columns_before = shifted(columns, "col", 1), shifted(columns, "col", -1)
+    slab_other, columns_after, columns_before, up_opposite, down_opposite = tied(
+        (slab_other, columns_after, columns_before, up_opposite, down_opposite)
+    )
+    with jax.named_scope("panel_columns"):
+        middle = TILE // 2
         columns_top = shifted(columns_after[:middle], "col", 1)
         columns_low = shifted(columns_before[middle:], "col", -1)
-        slab = jnp.concatenate(
-            [panel, panel_other, y_after, other_after, y_opposite, other_opposite]
-            + [y_before, other_before],
-            0,
-        )
-        slab_other = crossed(slab, "grp", 1)
-    slab_other, columns_top, columns_low, up_opposite, down_opposite, far_opposite = tied(
-        (slab_other, columns_top, columns_low, up_opposite, down_opposite, far_opposite)
-    )
-    with jax.named_scope("panel_columns"):
-        columns_opposite = jnp.concatenate([columns_top, columns_low], 0)
-        columns = jnp.stack([columns, columns_after, columns_opposite, columns_before])
-        columns_far = crossed(columns, "grp", 1)
-        columns_pair = crossed(columns[:, :, :wide], "grp", 2)
-        columns_far_pair = crossed(columns_pair, "grp", 1)
-        held = (columns, columns_pair, columns_far, columns_far_pair)
     with jax.named_scope("border_middle"):
         arrays = (own, x_after, x_before, x_opposite)
         arrays += (far, far_after, far_before, far_opposite)
@@ -267,34 +282,45 @@
         arrays += (z_before, down_after, down_before, down_opposite)
         parts = [(k, 0, full) for k in range(len(arrays))]
         mine, theirs = border_part(arrays, parts, full, root_places, slab, slab_other)
-        border = gather_rows(mine + crossed(theirs, "grp", 1))
+        border = mine + crossed(theirs, "grp", 1)
+        border, columns_top, columns_low = tied((border, columns_top, columns_low))
+        border = gather_rows(border)
+    with jax.named_scope("panel_columns"):
+        columns_opposite = jnp.concatenate([columns_top, columns_low], 0)
+        columns = jnp.stack([columns, columns_after, columns_opposite, columns_before])
+        columns_far = crossed(columns, "grp", 1)
+        columns_pair = crossed(columns, "grp", 2)
+        held = (columns, columns_pair, columns_far, crossed(columns_pair, "grp", 1))
     with jax.named_scope("inverse_middle"):
         spans = [(index, slot, 0) for index in range(4) for slot in range(4)]
         border_middle, inverse_middle = inverse_part(
             border, front, middle_spots, here, held, spans, pivot_middle, 3
         )
     with jax.named_scope("parent_rows"):
-        own = inverse_middle
-        full = own.shape[0]
-        half = full // 2
-        z_after, z_before = shifted(own, "col", 1), shifted(own, "col", -1)
-        pair = crossed(own, "grp", 2)
-        sides = jnp.concatenate([z_after, z_before], 0)
+        full = inverse_middle.shape[0]
+        lower_turned = lower_turned.T
+        packed = jnp.concatenate([lower_turned, inverse_middle], 0)
+        z_after, z_before = shifted(packed, "col", 1), shifted(packed, "col", -1)
+        pair = crossed(inverse_middle, "grp", 2)
+        sides = jnp.concatenate([z_after[TILE:], z_before[TILE:]], 0)
         sides_pair = crossed(sides, "grp", 2)
-        z_top = shifted(z_after[:half], "col", 1)
-        z_low = shifted(z_before[half:], "col", -1)
-        far = jnp.concatenate([z_top, z_low], 0)
+        z_top = shifted(z_after[: 2 * TILE], "col", 1)
+        z_low = shifted(z_before[2 * TILE :], "col", -1)
+        far = jnp.concatenate([z_top[TILE:], z_low], 0)
         far_pair = crossed(far, "grp", 2)
     with jax.named_scope("border_lower"):
-        arrays = (own, pair, z_after, sides_pair, far, far_pair, z_before)
+        arrays = (inverse_middle, pair, sides, sides_pair, far, far_pair)
         parts = [(0, 0, full), (1, 0, full), (2, 0, full), (3, 0, full)]
-        parts += [(4, 0, full), (5, 0, full), (6, 0, full), (3, full, full)]
+        parts += [(4, 0, full), (5, 0, full), (2, full, full), (3, full, full)]
         mine, theirs = border_part(arrays, parts, full, parent_places, slab, slab_other)
         border = gather_rows(mine + crossed(theirs, "grp", 1))
+    with jax.named_scope("lower_columns"):
+        lower_columns = jnp.stack([lower_turned, z_after[:TILE], z_top[:TILE], z_before[:TILE]])
+        lower_far = crossed(lower_columns, "grp", 1)
     with jax.named_scope("inverse_lower"):
-        spans = [(index, slot, wide) for index in range(2) for slot in range(4)]
+        spans = [(index, slot, 0) for index in range(2) for slot in range(4)]
         border_lower, inverse_lower = inverse_part(
-            border, lower, lower_spots, here, (columns, columns_far), spans, pivot_lower, 1
+            border, lower, lower_spots, here, (lower_columns, lower_far), spans, pivot_lower, 1
         )
     return (border_middle, inverse_middle, border_lower, inverse_lower)
 

time: 222 us -> 216 us (0.973); the launches traced: 217 us -> 216 us
  waiting for transfers between devices: 73.6 us -> 85.9 us
  Pallas kernels: 29.4 us -> 17.6 us
  local copies, waits for them, and re-layouts: 19.6 us -> 11.5 us
  starting transfers between devices: 87.2 us -> 91.5 us
    ppermute x30 -> x24, waiting for transfers between devices: 31.8 us -> 43.2 us  [shifted(): lax.ppermute(value, axis, [(i, (i - step) % size) for i in range(size)])]
    pallas_call x2, Pallas kernels: 21.6 us -> 10.4 us  [border_part(): pl.pallas_call(functools.partial(border_kernel, parts, len(arrays)), out_...]
    unnamed x72 -> x61, local copies, waits for them, and re-layouts: 13.2 us -> 3.78 us
    ppermute x30 -> x24, starting transfers between devices: 50.7 us -> 41.6 us  [shifted(): lax.ppermute(value, axis, [(i, (i - step) % size) for i in range(size)])]
    ppermute x1, starting transfers between devices: 5.07 us -> 13.6 us  [per_device(): lower_turned = lax.ppermute(panel_lower, AXES, swap_pairs(4))]
    all_to_all x0 -> x1, starting transfers between devices: none -> 4.33 us  [per_device(): lax.all_to_all(copies, 'row', 0, 0, tiled=True, axis_index_groups=same_z)]
    ppermute x1, waiting for transfers between devices: 0.01 us -> 3.94 us  [per_device(): turned = lax.ppermute(panel_middle, AXES, swap_pairs(2))]
    ppermute x10 -> x11, starting transfers between devices: 18.6 us -> 15 us  [crossed(): return lax.ppermute(value, axis, [(i, i ^ mask) for i in range(size)])]
  transfers between devices with their start and end apart: 44 -> 40, of which waited for: 17 -> 22; matrix products, arithmetic and copies ran while one was open for 7% -> 4% of each run, Pallas kernels for 0% -> 0%
where the time goes in v1:
time: 216 us
  starting transfers between devices  91.5 us (42%)
  waiting for transfers between devices  85.9 us (40%)
  Pallas kernels  17.6 us (8%)
  local copies, waits for them, and re-layouts  11.5 us (5%)
  other arithmetic  7.82 us (4%)
    ppermute x24, waiting for transfers between devices, shifted(): lax.ppermute(value, axis, [(i, (i - step) % size) for i in range(size)])  43.2 us
    ppermute x24, starting transfers between devices, shifted(): lax.ppermute(value, axis, [(i, (i - step) % size) for i in range(size)])  41.6 us
    ppermute x11, waiting for transfers between devices, crossed(): return lax.ppermute(value, axis, [(i, i ^ mask) for i in range(size)])  21.7 us
    all_to_all x2, waiting for transfers between devices, gather_rows(): got = lax.all_to_all(copies, 'row', 0, 0, tiled=True)  16 us
    ppermute x11, starting transfers between devices, crossed(): return lax.ppermute(value, axis, [(i, i ^ mask) for i in range(size)])  15 us
    ppermute x1, starting transfers between devices, per_device(): lower_turned = lax.ppermute(panel_lower, AXES, swap_pairs(4))  13.6 us
    pallas_call x2, Pallas kernels, border_part(): pl.pallas_call(functools.partial(border_kernel, parts, len(arrays)), out_...  10.4 us
    all_to_all x2, starting transfers between devices, gather_rows(): got = lax.all_to_all(copies, 'row', 0, 0, tiled=True)  9.36 us
  transfers between devices with their start and end apart: 40, of which 22 were waited for; matrix products, arithmetic and copies ran while one was open for 4% of the time, Pallas kernels for 0%

profile of v1, /device:TPU:1, one launch (start us, length us, event | category | flops | bytes accessed | tf_op | source)
XLA Modules:
  0.0 215.6 jit_solution(5110534535279863867)
XLA Ops:
  0.6 1.0 pad_maximum_fusion.2
  1.6 2.6 %collective-permute-start.4 = (f32[512,128]{1,0:T(8,128)S(1)}, f32[512,128]{1,0:T(8,128)S(1)}, u32[]{:S(2)}, u32[]{:S(2)}) collective-permute-start(f32[512,128]{1,0:T(8,128)S(1)} %pad_maximum_fusion.2), channel_id=1, source_target_pairs={{0,4},{4,0},{8,12},{12,8},{16,20},{20,16},{24,28},{28,24},{1,5},{5... | collective-permute-start | bytes 786440 | tf_op jit(solution)/shard_map/step_1/ppermute | solution.py:22
  4.2 5.1 %collective-permute-start = (f32[512,128]{1,0:T(8,128)}, f32[512,128]{1,0:T(8,128)S(1)}, u32[]{:S(2)}, u32[]{:S(2)}) collective-permute-start(f32[512,128]{1,0:T(8,128)} %refs_0_.1), channel_id=1, source_target_pairs={{0,3},{1,0},{2,1},{3,2},{4,7},{5,4},{6,5},{7,6},{8,11},{9,8},{10,9... | collective-permute-start | bytes 786440 | tf_op jit(solution)/shard_map/step_1/ppermute | solution.py:17
  9.3 2.5 %collective-permute-start.2 = (f32[512,128]{1,0:T(8,128)}, f32[512,128]{1,0:T(8,128)S(1)}, u32[]{:S(2)}, u32[]{:S(2)}) collective-permute-start(f32[512,128]{1,0:T(8,128)} %refs_0_.1), channel_id=1, source_target_pairs={{0,192},{32,224},{64,0},{96,32},{128,64},{160,96},{192,128},{224,1... | collective-permute-start | bytes 786440 | tf_op jit(solution)/shard_map/step_1/ppermute | solution.py:17
  11.8 1.0 pad_maximum_fusion.1
  12.8 1.8 collective-permute-done.refs_8_
  14.6 11.6 %collective-permute-done.1.refs_12_ = f32[512,128]{1,0:T(8,128)S(1)} collective-permute-done((f32[512,128]{1,0:T(8,128)}, f32[512,128]{1,0:T(8,128)S(1)}, u32[]{:S(2)}, u32[]{:S(2)}) %collective-permute-start.1) | collective-permute-done | bytes 262176 | tf_op jit(solution)/shard_map/step_1/ppermute | solution.py:17
  26.3 1.5 broadcast_in_dim.41
  27.8 4.3 %all-to-all-start = ((f32[4,1024,128]{2,1,0:T(8,128)}), f32[4,1024,128]{2,1,0:T(8,128)S(1)}, u32[]{:S(2)}, u32[]{:S(2)}) async-start(f32[4,1024,128]{2,1,0:T(8,128)} %broadcast_in_dim.41), calls=%async_computation | async-start | bytes 4194304 | tf_op jit(solution)/shard_map/step_2/all_to_all | solution.py:239
  32.2 1.2 collective-permute-start.5
  33.4 1.3 collective-permute-start.6
  34.7 2.5 %collective-permute-start.7 = (f32[512,128]{1,0:T(8,128)S(1)}, f32[512,128]{1,0:T(8,128)S(1)}, u32[]{:S(2)}, u32[]{:S(2)}) collective-permute-start(f32[512,128]{1,0:T(8,128)S(1)} %collective-permute-done.refs_8_), channel_id=1, source_target_pairs={{0,192},{32,224},{64,0},{96,32},{128,64},{160,96},{192,128},{224,1... | collective-permute-start | bytes 786440 | tf_op jit(solution)/shard_map/step_2/ppermute | solution.py:17
  37.2 2.7 %collective-permute-start.9 = (f32[512,128]{1,0:T(8,128)S(1)}, f32[512,128]{1,0:T(8,128)S(1)}, u32[]{:S(2)}, u32[]{:S(2)}) collective-permute-start(f32[512,128]{1,0:T(8,128)S(1)} %collective-permute-done.1.refs_12_), channel_id=1, source_target_pairs={{0,192},{32,224},{64,0},{96,32},{128,64},{160,96},{192,128},{224,1... | collective-permute-start | bytes 786440 | tf_op jit(solution)/shard_map/step_2/ppermute | solution.py:17
  39.9 0.8 collective-permute-done.6
  40.7 2.6 %collective-permute-start.11 = (f32[512,128]{1,0:T(8,128)S(1)}, f32[512,128]{1,0:T(8,128)}, u32[]{:S(2)}, u32[]{:S(2)}) collective-permute-start(f32[512,128]{1,0:T(8,128)S(1)} %constant_dynamic-update-slice_fusion.refs_4_), channel_id=1, source_target_pairs={{0,192},{32,224},{64,0},{96,32},{128,64},{160,96},{192,128},{224,1... | collective-permute-start | bytes 786440 | tf_op jit(solution)/shard_map/step_3/ppermute | solution.py:17
  43.9 1.2 collective-permute-start.13
  45.1 0.9 collective-permute-done.9.refs_13_
  46.0 3.4 %collective-permute-start.14 = (f32[512,128]{1,0:T(8,128)S(1)}, f32[512,128]{1,0:T(8,128)}, u32[]{:S(2)}, u32[]{:S(2)}) collective-permute-start(f32[512,128]{1,0:T(8,128)S(1)} %collective-permute-done.2.refs_1_), channel_id=1, source_target_pairs={{0,192},{32,224},{64,0},{96,32},{128,64},{160,96},{192,128},{224,1... | collective-permute-start | bytes 786440 | tf_op jit(solution)/shard_map/step_3/ppermute | solution.py:17
  49.5 13.6 %collective-permute-start.16 = (f32[128,128]{0,1:T(8,128)S(1)}, f32[128,128]{0,1:T(8,128)S(1)}, u32[]{:S(2)}, u32[]{:S(2)}) collective-permute-start(f32[128,128]{0,1:T(8,128)S(1)} %copy.16), channel_id=1, source_target_pairs={{0,0},{1,4},{2,8},{3,12},{4,1},{5,5},{6,9},{7,13},{8,2},{9,6},{10,... | collective-permute-start | bytes 196616 | tf_op jit(solution)/shard_map/step_3/ppermute | solution.py:255
  63.1 0.8 copy.15
  64.0 1.1 collective-permute-done.16
  65.1 7.6 %collective-permute-start.15 = (f32[384,128]{0,1:T(8,128)}, f32[384,128]{0,1:T(8,128)S(1)}, u32[]{:S(2)}, u32[]{:S(2)}) collective-permute-start(f32[384,128]{0,1:T(8,128)} %copy.15), channel_id=1, source_target_pairs={{0,0},{1,1},{2,4},{3,5},{4,2},{5,3},{6,6},{7,7},{8,32},{9,33},{10,... | collective-permute-start | bytes 589832 | tf_op jit(solution)/shard_map/step_3/ppermute | solution.py:254
  72.8 3.9 %collective-permute-done.15 = f32[384,128]{0,1:T(8,128)S(1)} collective-permute-done((f32[384,128]{0,1:T(8,128)}, f32[384,128]{0,1:T(8,128)S(1)}, u32[]{:S(2)}, u32[]{:S(2)}) %collective-permute-start.15) | collective-permute-done | bytes 196640 | tf_op jit(solution)/shard_map/step_3/ppermute | solution.py:254
  77.4 2.7 %collective-permute-start.21 = (f32[512,128]{1,0:T(8,128)}, f32[512,128]{1,0:T(8,128)}, u32[]{:S(2)}, u32[]{:S(2)}) collective-permute-start(f32[512,128]{1,0:T(8,128)} %collective-permute-done.10.refs_14_), channel_id=1, source_target_pairs={{0,64},{32,96},{64,128},{96,160},{128,192},{160,224},{192,0},{224,... | collective-permute-start | bytes 786440 | tf_op jit(solution)/shard_map/step_4/ppermute | solution.py:17
  80.8 7.5 %collective-permute-start.18 = (f32[128,384]{1,0:T(8,128)S(1)}, f32[128,384]{1,0:T(8,128)S(1)}, u32[]{:S(2)}, u32[]{:S(2)}) collective-permute-start(f32[128,384]{1,0:T(8,128)S(1)} %bitcast.49), channel_id=1, source_target_pairs={{0,3},{1,0},{2,1},{3,2},{4,7},{5,4},{6,5},{7,6},{8,11},{9,8},{10,9... | collective-permute-start | bytes 589832 | tf_op jit(solution)/shard_map/step_4/ppermute | solution.py:17
  88.9 7.1 %collective-permute-done.18 = f32[128,384]{1,0:T(8,128)S(1)} collective-permute-done((f32[128,384]{1,0:T(8,128)S(1)}, f32[128,384]{1,0:T(8,128)S(1)}, u32[]{:S(2)}, u32[]{:S(2)}) %collective-permute-start.18) | collective-permute-done | bytes 196640 | tf_op jit(solution)/shard_map/step_4/ppermute | solution.py:17
  96.1 3.0 %collective-permute-done.19 = f32[128,384]{1,0:T(8,128)S(1)} collective-permute-done((f32[128,384]{1,0:T(8,128)S(1)}, f32[128,384]{1,0:T(8,128)S(1)}, u32[]{:S(2)}, u32[]{:S(2)}) %collective-permute-start.19) | collective-permute-done | bytes 196640 | tf_op jit(solution)/shard_map/step_4/ppermute | solution.py:17
  99.1 0.7 copy-done.19
  99.8 6.7 %border_middle.1 = (f32[512,128]{1,0:T(8,128)}, f32[512,128]{1,0:T(8,128)}) custom-call(s32[16]{0:T(128)} %compare_select_fusion.8.places_ref, f32[512,128]{1,0:T(8,128)} %refs_0_.1, f32[512,128]{1,0:T(8,128)} %copy-done.13, f32[512,128]{1,0:T(8,128)} %copy-done.14, f32[512,128]{1,0:T(8,128)} %collective-permute-done.14.refs_3_, f32[512,128]{1,0:T(8,128)} %copy-done.10, ...), custom_call_target="tpu_custom_call" | custom-call | flops 1610612736 | bytes 33554432 | tf_op jit(solution)/shard_map/border_middle/pallas_call | solution.py:90
  106.5 2.1 collective-permute-start.22
  109.0 2.1 collective-permute-start.24
  111.1 1.0 add.335
  112.1 1.9 collective-permute-done.23
  114.0 1.3 collective-permute-done.24
  115.2 1.5 broadcast_in_dim.42
  116.7 5.8 %all-to-all-start.1 = ((f32[8,512,128]{2,1,0:T(8,128)}), f32[8,512,128]{2,1,0:T(8,128)S(1)}, u32[]{:S(2)}, u32[]{:S(2)}) async-start(f32[8,512,128]{2,1,0:T(8,128)} %broadcast_in_dim.42), calls=%async_computation.1 | async-start | bytes 4194304 | tf_op jit(solution)/shard_map/border_middle/all_to_all | solution.py:160
  122.5 1.0 pad_maximum_fusion.refs_0_
  124.4 1.4 collective-permute-start.26
  125.8 15.6 %collective-permute-done.25.refs_1_ = f32[4,128,384]{2,1,0:T(8,128)} collective-permute-done((f32[4,128,384]{2,1,0:T(8,128)S(1)}, f32[4,128,384]{2,1,0:T(8,128)}, u32[]{:S(2)}, u32[]{:S(2)}) %collective-permute-start.25) | collective-permute-done | bytes 786464 | tf_op jit(solution)/shard_map/panel_columns/ppermute | solution.py:22
  141.4 2.3 %collective-permute-start.27 = (f32[4,128,384]{2,1,0:T(8,128)}, f32[4,128,384]{2,1,0:T(8,128)}, u32[]{:S(2)}, u32[]{:S(2)}) collective-permute-start(f32[4,128,384]{2,1,0:T(8,128)} %collective-permute-done.25.refs_1_), channel_id=1, source_target_pairs={{0,32},{32,0},{64,96},{96,64},{128,160},{160,128},{192,224},{224,1... | collective-permute-start | bytes 2359304 | tf_op jit(solution)/shard_map/panel_columns/ppermute | solution.py:22
  144.6 1.3 collective-permute-done.27.refs_3_
  145.9 2.2 %all-to-all-done.1 = f32[8,512,128]{2,1,0:T(8,128)S(1)} async-done(((f32[8,512,128]{2,1,0:T(8,128)}), f32[8,512,128]{2,1,0:T(8,128)S(1)}, u32[]{:S(2)}, u32[]{:S(2)}) %all-to-all-start.1) | async-done | bytes 2097184 | tf_op jit(solution)/shard_map/border_middle/all_to_all | solution.py:160
  148.2 1.4 copy-done.2
  149.5 4.8 %inverse_middle.1 = (f32[384,128]{1,0:T(8,128)}, f32[256,128]{1,0:T(8,128)}) custom-call(s32[24]{0:T(128)} %copy-done.27, s32[16]{0:T(128)} %add.308.spots_ref, s32[1]{0:T(128)} %bitcast.5.where_ref, f32[4096,128]{1,0:T(8,128)} %bitcast.43, f32[4,128,384]{2,1,0:T(8,128)} %copy-done.4, f32[4,128,384]{2,1,0:T(8,128)} %collective-permute-done.25.refs_1_, ...), custom_call_target="tpu_custom_call" | custom-call | tf_op jit(solution)/shard_map/inverse_middle/pallas_call | solution.py:144
  154.3 0.9 pad_maximum_fusion.5
  155.2 2.0 collective-permute-start.30
  157.2 1.7 collective-permute-start.29
  159.5 0.7 collective-permute-start.28
  160.3 2.0 collective-permute-done.30
  162.2 6.7 %collective-permute-done.29 = f32[384,128]{1,0:T(8,128)S(1)} collective-permute-done((f32[384,128]{1,0:T(8,128)S(1)}, f32[384,128]{1,0:T(8,128)S(1)}, u32[]{:S(2)}, u32[]{:S(2)}) %collective-permute-start.29) | collective-permute-done | bytes 196640 | tf_op jit(solution)/shard_map/parent_rows/ppermute | solution.py:17
  168.9 0.8 collective-permute-start.31
  169.8 2.4 %collective-permute-start.32 = (f32[256,128]{1,0:T(8,128)S(1)}, f32[256,128]{1,0:T(8,128)S(1)}, u32[]{:S(2)}, u32[]{:S(2)}) collective-permute-start(f32[256,128]{1,0:T(8,128)S(1)} %get-tuple-element.86), channel_id=1, source_target_pairs={{0,3},{1,0},{2,1},{3,2},{4,7},{5,4},{6,5},{7,6},{8,11},{9,8},{10,9... | collective-permute-start | bytes 393224 | tf_op jit(solution)/shard_map/parent_rows/ppermute | solution.py:17
  172.3 3.4 %collective-permute-done.32 = f32[256,128]{1,0:T(8,128)S(1)} collective-permute-done((f32[256,128]{1,0:T(8,128)S(1)}, f32[256,128]{1,0:T(8,128)S(1)}, u32[]{:S(2)}, u32[]{:S(2)}) %collective-permute-start.32) | collective-permute-done | bytes 131104 | tf_op jit(solution)/shard_map/parent_rows/ppermute | solution.py:17
  175.7 2.2 %collective-permute-done.33 = f32[128,128]{1,0:T(8,128)S(1)} collective-permute-done((f32[128,128]{1,0:T(8,128)S(1)}, f32[128,128]{1,0:T(8,128)S(1)}, u32[]{:S(2)}, u32[]{:S(2)}) %collective-permute-start.33) | collective-permute-done | bytes 65568 | tf_op jit(solution)/shard_map/parent_rows/ppermute | solution.py:17
  178.7 3.1 %collective-permute-done.34.refs_5_ = f32[256,128]{1,0:T(8,128)S(1)} collective-permute-done((f32[256,128]{1,0:T(8,128)S(1)}, f32[256,128]{1,0:T(8,128)S(1)}, u32[]{:S(2)}, u32[]{:S(2)}) %collective-permute-start.34) | collective-permute-done | bytes 131104 | tf_op jit(solution)/shard_map/parent_rows/ppermute | solution.py:22
  182.4 3.7 %border_lower.1 = (f32[256,128]{1,0:T(8,128)}, f32[256,128]{1,0:T(8,128)}) custom-call(s32[8]{0:T(128)} %compare_select_fusion.12.places_ref, f32[256,128]{1,0:T(8,128)} %get-tuple-element.40.refs_0_, f32[256,128]{1,0:T(8,128)} %copy-done.25, f32[512,128]{1,0:T(8,128)} %copy-done.7, f32[512,128]{1,0:T(8,128)} %copy-done.23, f32[256,128]{1,0:T(8,128)} %copy-done.12, ...), custom_call_target="tpu_custom_call" | custom-call | flops 402653184 | bytes 8388608 | tf_op jit(solution)/shard_map/border_lower/pallas_call | solution.py:90
  186.2 3.8 %collective-permute-start.35 = (f32[256,128]{1,0:T(8,128)}, f32[256,128]{1,0:T(8,128)S(1)}, u32[]{:S(2)}, u32[]{:S(2)}) collective-permute-start(f32[256,128]{1,0:T(8,128)} %get-tuple-element.79), channel_id=1, source_target_pairs={{0,32},{32,0},{64,96},{96,64},{128,160},{160,128},{192,224},{224,1... | collective-permute-start | bytes 393224 | tf_op jit(solution)/shard_map/border_lower/ppermute | solution.py:22
  189.9 1.2 collective-permute-done.35
  191.1 0.9 add.354
  192.1 1.1 broadcast_in_dim.46
  193.1 3.6 %all-to-all-start.2 = ((f32[8,256,128]{2,1,0:T(8,128)}), f32[8,256,128]{2,1,0:T(8,128)S(1)}, u32[]{:S(2)}, u32[]{:S(2)}) async-start(f32[8,256,128]{2,1,0:T(8,128)} %broadcast_in_dim.46), calls=%async_computation.2 | async-start | bytes 2097152 | tf_op jit(solution)/shard_map/border_lower/all_to_all | solution.py:160
  198.4 13.8 %all-to-all-done.2 = f32[8,256,128]{2,1,0:T(8,128)S(1)} async-done(((f32[8,256,128]{2,1,0:T(8,128)}), f32[8,256,128]{2,1,0:T(8,128)S(1)}, u32[]{:S(2)}, u32[]{:S(2)}) %all-to-all-start.2) | async-done | bytes 1048608 | tf_op jit(solution)/shard_map/border_lower/all_to_all | solution.py:160
  212.2 1.0 copy-done.3
  213.1 2.4 %inverse_lower.1 = (f32[128,128]{1,0:T(8,128)}, f32[128,128]{1,0:T(8,128)}) custom-call(s32[8]{0:T(128)} %copy-done.28, s32[8]{0:T(128)} %add.340.spots_ref, s32[1]{0:T(128)} %bitcast.5.where_ref, f32[2048,128]{1,0:T(8,128)} %bitcast.44, f32[4,128,128]{2,1,0:T(8,128)} %copy-done.6, f32[4,128,128]{2,1,0:T(8,128)} %copy-done.20, f32[128,128]{1,0:T(8,128)} %refs_2_.1), custom_call_target="tpu_custom_call" | custom-call | tf_op jit(solution)/shard_map/inverse_lower/pallas_call | solution.py:144
  (135 shorter events, 8.8 us)
Async XLA Ops:
  0.6 143.8 %copy-start = (s32[4,8]{1,0:T(4,128)S(1)}, s32[4,8]{1,0:T(4,128)}, u32[]{:S(2)}) copy-start(s32[4,8]{1,0:T(4,128)} %param.13) | copy-start | bytes 388
  1.6 10.2 %collective-permute-start.4 = (f32[512,128]{1,0:T(8,128)S(1)}, f32[512,128]{1,0:T(8,128)S(1)}, u32[]{:S(2)}, u32[]{:S(2)}) collective-permute-start(f32[512,128]{1,0:T(8,128)S(1)} %pad_maximum_fusion.2), channel_id=1, source_target_pairs={{0,4},{4,0},{8,12},{12,8},{16,20},{20,16},{24,28},{28,24},{1,5},{5... | collective-permute-start | bytes 786440 | tf_op jit(solution)/shard_map/step_1/ppermute | solution.py:22
  4.2 10.5 %collective-permute-start = (f32[512,128]{1,0:T(8,128)}, f32[512,128]{1,0:T(8,128)S(1)}, u32[]{:S(2)}, u32[]{:S(2)}) collective-permute-start(f32[512,128]{1,0:T(8,128)} %refs_0_.1), channel_id=1, source_target_pairs={{0,3},{1,0},{2,1},{3,2},{4,7},{5,4},{6,5},{7,6},{8,11},{9,8},{10,9... | collective-permute-start | bytes 786440 | tf_op jit(solution)/shard_map/step_1/ppermute | solution.py:17
  9.3 16.9 %collective-permute-start.1 = (f32[512,128]{1,0:T(8,128)}, f32[512,128]{1,0:T(8,128)S(1)}, u32[]{:S(2)}, u32[]{:S(2)}) collective-permute-start(f32[512,128]{1,0:T(8,128)} %refs_0_.1), channel_id=1, source_target_pairs={{0,1},{1,2},{2,3},{3,0},{4,5},{5,6},{6,7},{7,4},{8,9},{9,10},{10,1... | collective-permute-start | bytes 786440 | tf_op jit(solution)/shard_map/step_1/ppermute | solution.py:17
  9.3 16.9 %collective-permute-start.2 = (f32[512,128]{1,0:T(8,128)}, f32[512,128]{1,0:T(8,128)S(1)}, u32[]{:S(2)}, u32[]{:S(2)}) collective-permute-start(f32[512,128]{1,0:T(8,128)} %refs_0_.1), channel_id=1, source_target_pairs={{0,192},{32,224},{64,0},{96,32},{128,64},{160,96},{192,128},{224,1... | collective-permute-start | bytes 786440 | tf_op jit(solution)/shard_map/step_1/ppermute | solution.py:17
  11.8 14.5 %collective-permute-start.3 = (f32[512,128]{1,0:T(8,128)}, f32[512,128]{1,0:T(8,128)S(1)}, u32[]{:S(2)}, u32[]{:S(2)}) collective-permute-start(f32[512,128]{1,0:T(8,128)} %refs_0_.1), channel_id=1, source_target_pairs={{0,64},{32,96},{64,128},{96,160},{128,192},{160,224},{192,0},{224,... | collective-permute-start | bytes 786440 | tf_op jit(solution)/shard_map/step_1/ppermute | solution.py:17
  14.6 22.5 %copy-start.8 = (f32[512,128]{1,0:T(8,128)}, f32[512,128]{1,0:T(8,128)S(1)}, u32[]{:S(2)}) copy-start(f32[512,128]{1,0:T(8,128)S(1)} %collective-permute-done.refs_8_) | copy-start | bytes 786436
  26.3 13.6 %copy-start.9 = (f32[512,128]{1,0:T(8,128)}, f32[512,128]{1,0:T(8,128)S(1)}, u32[]{:S(2)}) copy-start(f32[512,128]{1,0:T(8,128)S(1)} %collective-permute-done.1.refs_12_) | copy-start | bytes 786436
  26.3 19.7 %copy-start.13 = (f32[512,128]{1,0:T(8,128)}, f32[512,128]{1,0:T(8,128)S(1)}, u32[]{:S(2)}) copy-start(f32[512,128]{1,0:T(8,128)S(1)} %collective-permute-done.2.refs_1_) | copy-start | bytes 786436
  27.8 21.6 %copy-start.11 = (f32[128,128]{1,0:T(8,128)S(1)}, f32[128,128]{1,0:T(8,128)}, u32[]{:S(2)}) copy-start(f32[128,128]{1,0:T(8,128)} %param.10) | copy-start | bytes 196612
  27.8 35.3 %copy-start.5 = (f32[384,128]{1,0:T(8,128)S(1)}, f32[384,128]{1,0:T(8,128)}, u32[]{:S(2)}) copy-start(f32[384,128]{1,0:T(8,128)} %param.8) | copy-start | bytes 589828
  27.8 49.3 %copy-start.29 = (s32[2,24]{1,0:T(2,128)S(1)}, s32[2,24]{1,0:T(2,128)}, u32[]{:S(2)}) copy-start(s32[2,24]{1,0:T(2,128)} %param.12) | copy-start | bytes 580
  27.8 48.9 %all-to-all-start = ((f32[4,1024,128]{2,1,0:T(8,128)}), f32[4,1024,128]{2,1,0:T(8,128)S(1)}, u32[]{:S(2)}, u32[]{:S(2)}) async-start(f32[4,1024,128]{2,1,0:T(8,128)} %broadcast_in_dim.41), calls=%async_computation | async-start | bytes 4194304 | tf_op jit(solution)/shard_map/step_2/all_to_all | solution.py:239
  32.2 7.7 %collective-permute-start.5 = (f32[256,128]{1,0:T(8,128)S(1)}, f32[256,128]{1,0:T(8,128)S(1)}, u32[]{:S(2)}, u32[]{:S(2)}) collective-permute-start(f32[256,128]{1,0:T(8,128)S(1)} %slice.36), channel_id=1, source_target_pairs={{0,3},{1,0},{2,1},{3,2},{4,7},{5,4},{6,5},{7,6},{8,11},{9,8},{10,9... | collective-permute-start | bytes 393224 | tf_op jit(solution)/shard_map/step_2/ppermute | solution.py:17
  33.4 7.3 %collective-permute-start.6 = (f32[256,128]{1,0:T(8,128)S(1)}, f32[256,128]{1,0:T(8,128)S(1)}, u32[]{:S(2)}, u32[]{:S(2)}) collective-permute-start(f32[256,128]{1,0:T(8,128)S(1)} %slice.37), channel_id=1, source_target_pairs={{0,1},{1,2},{2,3},{3,0},{4,5},{5,6},{6,7},{7,4},{8,9},{9,10},{10,1... | collective-permute-start | bytes 393224 | tf_op jit(solution)/shard_map/step_2/ppermute | solution.py:17
  34.7 8.6 %collective-permute-start.7 = (f32[512,128]{1,0:T(8,128)S(1)}, f32[512,128]{1,0:T(8,128)S(1)}, u32[]{:S(2)}, u32[]{:S(2)}) collective-permute-start(f32[512,128]{1,0:T(8,128)S(1)} %collective-permute-done.refs_8_), channel_id=1, source_target_pairs={{0,192},{32,224},{64,0},{96,32},{128,64},{160,96},{192,128},{224,1... | collective-permute-start | bytes 786440 | tf_op jit(solution)/shard_map/step_2/ppermute | solution.py:17
  37.2 6.7 %collective-permute-start.8 = (f32[512,128]{1,0:T(8,128)S(1)}, f32[512,128]{1,0:T(8,128)S(1)}, u32[]{:S(2)}, u32[]{:S(2)}) collective-permute-start(f32[512,128]{1,0:T(8,128)S(1)} %collective-permute-done.refs_8_), channel_id=1, source_target_pairs={{0,64},{32,96},{64,128},{96,160},{128,192},{160,224},{192,0},{224,... | collective-permute-start | bytes 786440 | tf_op jit(solution)/shard_map/step_2/ppermute | solution.py:17
  37.2 8.8 %collective-permute-start.9 = (f32[512,128]{1,0:T(8,128)S(1)}, f32[512,128]{1,0:T(8,128)S(1)}, u32[]{:S(2)}, u32[]{:S(2)}) collective-permute-start(f32[512,128]{1,0:T(8,128)S(1)} %collective-permute-done.1.refs_12_), channel_id=1, source_target_pairs={{0,192},{32,224},{64,0},{96,32},{128,64},{160,96},{192,128},{224,1... | collective-permute-start | bytes 786440 | tf_op jit(solution)/shard_map/step_2/ppermute | solution.py:17
  39.9 9.6 %collective-permute-start.10 = (f32[512,128]{1,0:T(8,128)S(1)}, f32[512,128]{1,0:T(8,128)}, u32[]{:S(2)}, u32[]{:S(2)}) collective-permute-start(f32[512,128]{1,0:T(8,128)S(1)} %collective-permute-done.1.refs_12_), channel_id=1, source_target_pairs={{0,64},{32,96},{64,128},{96,160},{128,192},{160,224},{192,0},{224,... | collective-permute-start | bytes 786440 | tf_op jit(solution)/shard_map/step_2/ppermute | solution.py:17
  40.7 58.3 %copy-start.10 = (f32[512,128]{1,0:T(8,128)}, f32[512,128]{1,0:T(8,128)S(1)}, u32[]{:S(2)}) copy-start(f32[512,128]{1,0:T(8,128)S(1)} %constant_dynamic-update-slice_fusion.refs_4_) | copy-start | bytes 786436
  40.7 32.0 %collective-permute-start.11 = (f32[512,128]{1,0:T(8,128)S(1)}, f32[512,128]{1,0:T(8,128)}, u32[]{:S(2)}, u32[]{:S(2)}) collective-permute-start(f32[512,128]{1,0:T(8,128)S(1)} %constant_dynamic-update-slice_fusion.refs_4_), channel_id=1, source_target_pairs={{0,192},{32,224},{64,0},{96,32},{128,64},{160,96},{192,128},{224,1... | collective-permute-start | bytes 786440 | tf_op jit(solution)/shard_map/step_3/ppermute | solution.py:17
  43.3 6.1 %copy-start.15 = (f32[512,128]{1,0:T(8,128)}, f32[512,128]{1,0:T(8,128)S(1)}, u32[]{:S(2)}) copy-start(f32[512,128]{1,0:T(8,128)S(1)} %collective-permute-done.7.refs_9_) | copy-start | bytes 786436
  43.3 29.4 %collective-permute-start.12 = (f32[512,128]{1,0:T(8,128)S(1)}, f32[512,128]{1,0:T(8,128)}, u32[]{:S(2)}, u32[]{:S(2)}) collective-permute-start(f32[512,128]{1,0:T(8,128)S(1)} %constant_dynamic-update-slice_fusion.refs_4_), channel_id=1, source_target_pairs={{0,64},{32,96},{64,128},{96,160},{128,192},{160,224},{192,0},{224,... | collective-permute-start | bytes 786440 | tf_op jit(solution)/shard_map/step_3/ppermute | solution.py:17
  43.9 5.5 %copy-start.16 = (f32[512,128]{1,0:T(8,128)}, f32[512,128]{1,0:T(8,128)S(1)}, u32[]{:S(2)}) copy-start(f32[512,128]{1,0:T(8,128)S(1)} %collective-permute-done.8.refs_10_) | copy-start | bytes 786436
  43.9 28.8 %collective-permute-start.13 = (f32[512,128]{1,0:T(8,128)S(1)}, f32[512,128]{1,0:T(8,128)S(1)}, u32[]{:S(2)}, u32[]{:S(2)}) collective-permute-start(f32[512,128]{1,0:T(8,128)S(1)} %constant_dynamic-update-slice_fusion.refs_4_), channel_id=1, source_target_pairs={{0,128},{32,160},{64,192},{96,224},{128,0},{160,32},{192,64},{224,... | collective-permute-start | bytes 786440 | tf_op jit(solution)/shard_map/step_3/ppermute | solution.py:17
  46.0 3.4 %copy-start.17 = (f32[512,128]{1,0:T(8,128)}, f32[512,128]{1,0:T(8,128)S(1)}, u32[]{:S(2)}) copy-start(f32[512,128]{1,0:T(8,128)S(1)} %collective-permute-done.9.refs_13_) | copy-start | bytes 786436
  46.0 26.7 %collective-permute-start.14 = (f32[512,128]{1,0:T(8,128)S(1)}, f32[512,128]{1,0:T(8,128)}, u32[]{:S(2)}, u32[]{:S(2)}) collective-permute-start(f32[512,128]{1,0:T(8,128)S(1)} %collective-permute-done.2.refs_1_), channel_id=1, source_target_pairs={{0,192},{32,224},{64,0},{96,32},{128,64},{160,96},{192,128},{224,1... | collective-permute-start | bytes 786440 | tf_op jit(solution)/shard_map/step_3/ppermute | solution.py:17
  49.5 15.5 %collective-permute-start.16 = (f32[128,128]{0,1:T(8,128)S(1)}, f32[128,128]{0,1:T(8,128)S(1)}, u32[]{:S(2)}, u32[]{:S(2)}) collective-permute-start(f32[128,128]{0,1:T(8,128)S(1)} %copy.16), channel_id=1, source_target_pairs={{0,0},{1,4},{2,8},{3,12},{4,1},{5,5},{6,9},{7,13},{8,2},{9,6},{10,... | collective-permute-start | bytes 196616 | tf_op jit(solution)/shard_map/step_3/ppermute | solution.py:255
  65.1 12.1 %copy-start.21 = (f32[128,128]{0,1:T(8,128)}, f32[128,128]{0,1:T(8,128)S(1)}, u32[]{:S(2)}) copy-start(f32[128,128]{0,1:T(8,128)S(1)} %collective-permute-done.16) | copy-start | bytes 196612
  65.1 11.6 %collective-permute-start.15 = (f32[384,128]{0,1:T(8,128)}, f32[384,128]{0,1:T(8,128)S(1)}, u32[]{:S(2)}, u32[]{:S(2)}) collective-permute-start(f32[384,128]{0,1:T(8,128)} %copy.15), channel_id=1, source_target_pairs={{0,0},{1,1},{2,4},{3,5},{4,2},{5,3},{6,6},{7,7},{8,32},{9,33},{10,... | collective-permute-start | bytes 589832 | tf_op jit(solution)/shard_map/step_3/ppermute | solution.py:254
  72.7 26.3 %copy-start.18 = (f32[512,128]{1,0:T(8,128)}, f32[512,128]{1,0:T(8,128)S(1)}, u32[]{:S(2)}) copy-start(f32[512,128]{1,0:T(8,128)S(1)} %collective-permute-done.13.refs_7_) | copy-start | bytes 786436
  76.7 29.7 %copy-start.24 = (f32[384,128]{0,1:T(8,128)}, f32[384,128]{0,1:T(8,128)S(1)}, u32[]{:S(2)}) copy-start(f32[384,128]{0,1:T(8,128)S(1)} %collective-permute-done.15) | copy-start | bytes 589828
  76.7 22.4 %copy-start.1 = (f32[4,1024,128]{2,1,0:T(8,128)}, f32[4,1024,128]{2,1,0:T(8,128)S(1)}, u32[]{:S(2)}) copy-start(f32[4,1024,128]{2,1,0:T(8,128)S(1)} %all-to-all-done) | copy-start | bytes 6291460
  76.7 22.3 %collective-permute-start.17 = (f32[4096,128]{1,0:T(8,128)S(1)}, f32[4096,128]{1,0:T(8,128)}, u32[]{:S(2)}, u32[]{:S(2)}) collective-permute-start(f32[4096,128]{1,0:T(8,128)S(1)} %bitcast.40), channel_id=1, source_target_pairs={{0,32},{32,0},{64,96},{96,64},{128,160},{160,128},{192,224},{224,1... | collective-permute-start | bytes 6291464 | tf_op jit(solution)/shard_map/step_4/ppermute | solution.py:22
  77.1 29.4 %copy-start.27 = (s32[24]{0:T(128)}, s32[24]{0:T(128)S(1)}, u32[]{:S(2)}) copy-start(s32[24]{0:T(128)S(1)} %dynamic-slice_bitcast_fusion.1.tiles_ref) | copy-start | bytes 292
  77.2 21.8 %collective-permute-start.20 = (f32[512,128]{1,0:T(8,128)}, f32[512,128]{1,0:T(8,128)S(1)}, u32[]{:S(2)}, u32[]{:S(2)}) collective-permute-start(f32[512,128]{1,0:T(8,128)} %copy-done.15), channel_id=1, source_target_pairs={{0,192},{32,224},{64,0},{96,32},{128,64},{160,96},{192,128},{224,1... | collective-permute-start | bytes 786440 | tf_op jit(solution)/shard_map/step_4/ppermute | solution.py:17
  77.4 21.6 %collective-permute-start.21 = (f32[512,128]{1,0:T(8,128)}, f32[512,128]{1,0:T(8,128)}, u32[]{:S(2)}, u32[]{:S(2)}) collective-permute-start(f32[512,128]{1,0:T(8,128)} %collective-permute-done.10.refs_14_), channel_id=1, source_target_pairs={{0,64},{32,96},{64,128},{96,160},{128,192},{160,224},{192,0},{224,... | collective-permute-start | bytes 786440 | tf_op jit(solution)/shard_map/step_4/ppermute | solution.py:17
  80.8 15.2 %collective-permute-start.18 = (f32[128,384]{1,0:T(8,128)S(1)}, f32[128,384]{1,0:T(8,128)S(1)}, u32[]{:S(2)}, u32[]{:S(2)}) collective-permute-start(f32[128,384]{1,0:T(8,128)S(1)} %bitcast.49), channel_id=1, source_target_pairs={{0,3},{1,0},{2,1},{3,2},{4,7},{5,4},{6,5},{7,6},{8,11},{9,8},{10,9... | collective-permute-start | bytes 589832 | tf_op jit(solution)/shard_map/step_4/ppermute | solution.py:17
  88.4 10.6 %collective-permute-start.19 = (f32[128,384]{1,0:T(8,128)S(1)}, f32[128,384]{1,0:T(8,128)S(1)}, u32[]{:S(2)}, u32[]{:S(2)}) collective-permute-start(f32[128,384]{1,0:T(8,128)S(1)} %bitcast.50), channel_id=1, source_target_pairs={{0,1},{1,2},{2,3},{3,0},{4,5},{5,6},{6,7},{7,4},{8,9},{9,10},{10,1... | collective-permute-start | bytes 589832 | tf_op jit(solution)/shard_map/step_4/ppermute | solution.py:17
  106.5 4.6 %collective-permute-start.22 = (f32[512,128]{1,0:T(8,128)}, f32[512,128]{1,0:T(8,128)S(1)}, u32[]{:S(2)}, u32[]{:S(2)}) collective-permute-start(f32[512,128]{1,0:T(8,128)} %get-tuple-element.69), channel_id=1, source_target_pairs={{0,32},{32,0},{64,96},{96,64},{128,160},{160,128},{192,224},{224,1... | collective-permute-start | bytes 786440 | tf_op jit(solution)/shard_map/border_middle/ppermute | solution.py:22
  108.6 5.4 %collective-permute-start.23 = (f32[64,384]{1,0:T(8,128)S(1)}, f32[64,384]{1,0:T(8,128)S(1)}, u32[]{:S(2)}, u32[]{:S(2)}) collective-permute-start(f32[64,384]{1,0:T(8,128)S(1)} %slice.38), channel_id=1, source_target_pairs={{0,3},{1,0},{2,1},{3,2},{4,7},{5,4},{6,5},{7,6},{8,11},{9,8},{10,9... | collective-permute-start | bytes 294920 | tf_op jit(solution)/shard_map/panel_columns/ppermute | solution.py:17
  109.0 6.3 %collective-permute-start.24 = (f32[64,384]{1,0:T(8,128)S(1)}, f32[64,384]{1,0:T(8,128)S(1)}, u32[]{:S(2)}, u32[]{:S(2)}) collective-permute-start(f32[64,384]{1,0:T(8,128)S(1)} %slice.39), channel_id=1, source_target_pairs={{0,1},{1,2},{2,3},{3,0},{4,5},{5,6},{6,7},{7,4},{8,9},{9,10},{10,1... | collective-permute-start | bytes 294920 | tf_op jit(solution)/shard_map/panel_columns/ppermute | solution.py:17
  116.7 31.5 %all-to-all-start.1 = ((f32[8,512,128]{2,1,0:T(8,128)}), f32[8,512,128]{2,1,0:T(8,128)S(1)}, u32[]{:S(2)}, u32[]{:S(2)}) async-start(f32[8,512,128]{2,1,0:T(8,128)} %broadcast_in_dim.42), calls=%async_computation.1 | async-start | bytes 4194304 | tf_op jit(solution)/shard_map/border_middle/all_to_all | solution.py:160
  123.5 24.6 %copy-start.4 = (f32[4,128,384]{2,1,0:T(8,128)}, f32[4,128,384]{2,1,0:T(8,128)S(1)}, u32[]{:S(2)}) copy-start(f32[4,128,384]{2,1,0:T(8,128)S(1)} %pad_maximum_fusion.refs_0_) | copy-start | bytes 2359300
  123.5 17.9 %collective-permute-start.25 = (f32[4,128,384]{2,1,0:T(8,128)S(1)}, f32[4,128,384]{2,1,0:T(8,128)}, u32[]{:S(2)}, u32[]{:S(2)}) collective-permute-start(f32[4,128,384]{2,1,0:T(8,128)S(1)} %pad_maximum_fusion.refs_0_), channel_id=1, source_target_pairs={{0,64},{32,96},{64,0},{96,32},{128,192},{160,224},{192,128},{224,1... | collective-permute-start | bytes 2359304 | tf_op jit(solution)/shard_map/panel_columns/ppermute | solution.py:22
  124.4 20.2 %collective-permute-start.26 = (f32[4,128,384]{2,1,0:T(8,128)S(1)}, f32[4,128,384]{2,1,0:T(8,128)}, u32[]{:S(2)}, u32[]{:S(2)}) collective-permute-start(f32[4,128,384]{2,1,0:T(8,128)S(1)} %pad_maximum_fusion.refs_0_), channel_id=1, source_target_pairs={{0,32},{32,0},{64,96},{96,64},{128,160},{160,128},{192,224},{224,1... | collective-permute-start | bytes 2359304 | tf_op jit(solution)/shard_map/panel_columns/ppermute | solution.py:22
  141.4 4.5 %collective-permute-start.27 = (f32[4,128,384]{2,1,0:T(8,128)}, f32[4,128,384]{2,1,0:T(8,128)}, u32[]{:S(2)}, u32[]{:S(2)}) collective-permute-start(f32[4,128,384]{2,1,0:T(8,128)} %collective-permute-done.25.refs_1_), channel_id=1, source_target_pairs={{0,32},{32,0},{64,96},{96,64},{128,160},{160,128},{192,224},{224,1... | collective-permute-start | bytes 2359304 | tf_op jit(solution)/shard_map/panel_columns/ppermute | solution.py:22
  144.5 9.8 %copy-start.28 = (s32[8]{0:T(128)}, s32[8]{0:T(128)S(1)}, u32[]{:S(2)}) copy-start(s32[8]{0:T(128)S(1)} %dynamic-slice_bitcast_fusion.tiles_ref) | copy-start | bytes 100
  149.5 4.8 %copy-start.22 = (f32[128,128]{0,1:T(8,128)S(1)}, f32[128,128]{0,1:T(8,128)}, u32[]{:S(2)}) copy-start(f32[128,128]{0,1:T(8,128)} %copy-done.21) | copy-start | bytes 196612
  155.2 7.0 %collective-permute-start.30 = (f32[384,128]{1,0:T(8,128)S(1)}, f32[384,128]{1,0:T(8,128)S(1)}, u32[]{:S(2)}, u32[]{:S(2)}) collective-permute-start(f32[384,128]{1,0:T(8,128)S(1)} %pad_maximum_fusion.5), channel_id=1, source_target_pairs={{0,1},{1,2},{2,3},{3,0},{4,5},{5,6},{6,7},{7,4},{8,9},{9,10},{10,1... | collective-permute-start | bytes 589832 | tf_op jit(solution)/shard_map/parent_rows/ppermute | solution.py:17
  157.2 11.7 %collective-permute-start.29 = (f32[384,128]{1,0:T(8,128)S(1)}, f32[384,128]{1,0:T(8,128)S(1)}, u32[]{:S(2)}, u32[]{:S(2)}) collective-permute-start(f32[384,128]{1,0:T(8,128)S(1)} %pad_maximum_fusion.5), channel_id=1, source_target_pairs={{0,3},{1,0},{2,1},{3,2},{4,7},{5,4},{6,5},{7,6},{8,11},{9,8},{10,9... | collective-permute-start | bytes 589832 | tf_op jit(solution)/shard_map/parent_rows/ppermute | solution.py:17
  159.5 19.1 %collective-permute-start.28 = (f32[256,128]{1,0:T(8,128)}, f32[256,128]{1,0:T(8,128)S(1)}, u32[]{:S(2)}, u32[]{:S(2)}) collective-permute-start(f32[256,128]{1,0:T(8,128)} %get-tuple-element.40.refs_0_), channel_id=1, source_target_pairs={{0,64},{32,96},{64,0},{96,32},{128,192},{160,224},{192,128},{224,1... | collective-permute-start | bytes 393224 | tf_op jit(solution)/shard_map/parent_rows/ppermute | solution.py:22
  168.9 12.8 %copy-start.7 = (f32[512,128]{1,0:T(8,128)}, f32[512,128]{1,0:T(8,128)S(1)}, u32[]{:S(2)}) copy-start(f32[512,128]{1,0:T(8,128)S(1)} %pad_maximum_fusion.3.refs_2_) | copy-start | bytes 786436
  168.9 9.7 %collective-permute-start.31 = (f32[512,128]{1,0:T(8,128)S(1)}, f32[512,128]{1,0:T(8,128)S(1)}, u32[]{:S(2)}, u32[]{:S(2)}) collective-permute-start(f32[512,128]{1,0:T(8,128)S(1)} %pad_maximum_fusion.3.refs_2_), channel_id=1, source_target_pairs={{0,64},{32,96},{64,0},{96,32},{128,192},{160,224},{192,128},{224,1... | collective-permute-start | bytes 786440 | tf_op jit(solution)/shard_map/parent_rows/ppermute | solution.py:22
  169.8 5.9 %collective-permute-start.32 = (f32[256,128]{1,0:T(8,128)S(1)}, f32[256,128]{1,0:T(8,128)S(1)}, u32[]{:S(2)}, u32[]{:S(2)}) collective-permute-start(f32[256,128]{1,0:T(8,128)S(1)} %get-tuple-element.86), channel_id=1, source_target_pairs={{0,3},{1,0},{2,1},{3,2},{4,7},{5,4},{6,5},{7,6},{8,11},{9,8},{10,9... | collective-permute-start | bytes 393224 | tf_op jit(solution)/shard_map/parent_rows/ppermute | solution.py:17
  172.2 5.7 %collective-permute-start.33 = (f32[128,128]{1,0:T(8,128)S(1)}, f32[128,128]{1,0:T(8,128)S(1)}, u32[]{:S(2)}, u32[]{:S(2)}) collective-permute-start(f32[128,128]{1,0:T(8,128)S(1)} %get-tuple-element.85), channel_id=1, source_target_pairs={{0,1},{1,2},{2,3},{3,0},{4,5},{5,6},{6,7},{7,4},{8,9},{9,10},{10,1... | collective-permute-start | bytes 196616 | tf_op jit(solution)/shard_map/parent_rows/ppermute | solution.py:17
  177.9 3.9 %copy-start.12 = (f32[256,128]{1,0:T(8,128)}, f32[256,128]{1,0:T(8,128)S(1)}, u32[]{:S(2)}) copy-start(f32[256,128]{1,0:T(8,128)S(1)} %pad_maximum_fusion.6.refs_4_) | copy-start | bytes 393220
  177.9 3.9 %collective-permute-start.34 = (f32[256,128]{1,0:T(8,128)S(1)}, f32[256,128]{1,0:T(8,128)S(1)}, u32[]{:S(2)}, u32[]{:S(2)}) collective-permute-start(f32[256,128]{1,0:T(8,128)S(1)} %pad_maximum_fusion.6.refs_4_), channel_id=1, source_target_pairs={{0,64},{32,96},{64,0},{96,32},{128,192},{160,224},{192,128},{224,1... | collective-permute-start | bytes 393224 | tf_op jit(solution)/shard_map/parent_rows/ppermute | solution.py:22
  178.7 3.1 %copy-start.25 = (f32[256,128]{1,0:T(8,128)}, f32[256,128]{1,0:T(8,128)S(1)}, u32[]{:S(2)}) copy-start(f32[256,128]{1,0:T(8,128)S(1)} %collective-permute-done.28.refs_1_) | copy-start | bytes 393220
  186.2 5.0 %collective-permute-start.35 = (f32[256,128]{1,0:T(8,128)}, f32[256,128]{1,0:T(8,128)S(1)}, u32[]{:S(2)}, u32[]{:S(2)}) collective-permute-start(f32[256,128]{1,0:T(8,128)} %get-tuple-element.79), channel_id=1, source_target_pairs={{0,32},{32,0},{64,96},{96,64},{128,160},{160,128},{192,224},{224,1... | collective-permute-start | bytes 393224 | tf_op jit(solution)/shard_map/border_lower/ppermute | solution.py:22
  193.1 19.0 %all-to-all-start.2 = ((f32[8,256,128]{2,1,0:T(8,128)}), f32[8,256,128]{2,1,0:T(8,128)S(1)}, u32[]{:S(2)}, u32[]{:S(2)}) async-start(f32[8,256,128]{2,1,0:T(8,128)} %broadcast_in_dim.46), calls=%async_computation.2 | async-start | bytes 2097152 | tf_op jit(solution)/shard_map/border_lower/all_to_all | solution.py:160
  196.7 15.4 %copy-start.6 = (f32[4,128,128]{2,1,0:T(8,128)}, f32[4,128,128]{2,1,0:T(8,128)S(1)}, u32[]{:S(2)}) copy-start(f32[4,128,128]{2,1,0:T(8,128)S(1)} %pad_maximum_fusion.4.refs_0_) | copy-start | bytes 786436
  196.8 1.6 collective-permute-start.36
  198.4 13.8 %copy-start.20 = (f32[4,128,128]{2,1,0:T(8,128)}, f32[4,128,128]{2,1,0:T(8,128)S(1)}, u32[]{:S(2)}) copy-start(f32[4,128,128]{2,1,0:T(8,128)S(1)} %collective-permute-done.36.refs_1_) | copy-start | bytes 786436
  (6 other events, 8.4 us)

commit v2 on v1

--- a/solution.py
+++ b/solution.py
@@ -304,18 +304,16 @@
         pair = crossed(inverse_middle, "grp", 2)
         sides = jnp.concatenate([z_after[TILE:], z_before[TILE:]], 0)
         sides_pair = crossed(sides, "grp", 2)
-        z_top = shifted(z_after[: 2 * TILE], "col", 1)
-        z_low = shifted(z_before[2 * TILE :], "col", -1)
-        far = jnp.concatenate([z_top[TILE:], z_low], 0)
-        far_pair = crossed(far, "grp", 2)
+        opposite = shifted(z_after, "col", 1)
+        far_pair = crossed(opposite[TILE:], "grp", 2)
     with jax.named_scope("border_lower"):
-        arrays = (inverse_middle, pair, sides, sides_pair, far, far_pair)
+        arrays = (inverse_middle, pair, sides, sides_pair, opposite, far_pair)
         parts = [(0, 0, full), (1, 0, full), (2, 0, full), (3, 0, full)]
-        parts += [(4, 0, full), (5, 0, full), (2, full, full), (3, full, full)]
+        parts += [(4, TILE, full), (5, 0, full), (2, full, full), (3, full, full)]
         mine, theirs = border_part(arrays, parts, full, parent_places, slab, slab_other)
         border = gather_rows(mine + crossed(theirs, "grp", 1))
     with jax.named_scope("lower_columns"):
-        lower_columns = jnp.stack([lower_turned, z_after[:TILE], z_top[:TILE], z_before[:TILE]])
+        lower_columns = jnp.stack([lower_turned, z_after[:TILE], opposite[:TILE], z_before[:TILE]])
         lower_far = crossed(lower_columns, "grp", 1)
     with jax.named_scope("inverse_lower"):
         spans = [(index, slot, 0) for index in range(2) for slot in range(4)]

time: 216 us -> 216 us (level)
    ppermute x24 -> x23, waiting for transfers between devices: 43.2 us -> 44.6 us  [shifted(): lax.ppermute(value, axis, [(i, (i - step) % size) for i in range(size)])]
    ppermute x24 -> x23, starting transfers between devices: 41.6 us -> 41.4 us  [shifted(): lax.ppermute(value, axis, [(i, (i - step) % size) for i in range(size)])]
  transfers between devices with their start and end apart: 40 -> 39, of which waited for: 22 -> 21; matrix products, arithmetic and copies ran while one was open for 4% -> 4% of each run, Pallas kernels for 0% -> 0%
where the time goes in v2:
time: 216 us; the launch traced here: 215 us
  starting transfers between devices  91.2 us (42%)
  waiting for transfers between devices  87.8 us (41%)
  Pallas kernels  17.1 us (8%)
  local copies, waits for them, and re-layouts  10.5 us (5%)
  other arithmetic  7.83 us (4%)
    ppermute x23, waiting for transfers between devices, shifted(): lax.ppermute(value, axis, [(i, (i - step) % size) for i in range(size)])  44.6 us
    ppermute x23, starting transfers between devices, shifted(): lax.ppermute(value, axis, [(i, (i - step) % size) for i in range(size)])  41.4 us
    ppermute x11, waiting for transfers between devices, crossed(): return lax.ppermute(value, axis, [(i, i ^ mask) for i in range(size)])  22.7 us
    all_to_all x2, waiting for transfers between devices, gather_rows(): got = lax.all_to_all(copies, 'row', 0, 0, tiled=True)  15.1 us
    ppermute x11, starting transfers between devices, crossed(): return lax.ppermute(value, axis, [(i, i ^ mask) for i in range(size)])  14.1 us
    ppermute x1, starting transfers between devices, per_device(): lower_turned = lax.ppermute(panel_lower, AXES, swap_pairs(4))  13.6 us
    all_to_all x2, starting transfers between devices, gather_rows(): got = lax.all_to_all(copies, 'row', 0, 0, tiled=True)  10.1 us
    pallas_call x2, Pallas kernels, border_part(): pl.pallas_call(functools.partial(border_kernel, parts, len(arrays)), out_...  9.91 us
  transfers between devices with their start and end apart: 39, of which 21 were waited for; matrix products, arithmetic and copies ran while one was open for 4% of the time, Pallas kernels for 0%

profile of v2, /device:TPU:1, one launch (start us, length us, event | category | flops | bytes accessed | tf_op | source)
XLA Modules:
  0.0 215.5 jit_solution(16703110237537862372)
XLA Ops:
  0.6 1.0 pad_maximum_fusion.2
  1.6 2.6 %collective-permute-start.4 = (f32[512,128]{1,0:T(8,128)S(1)}, f32[512,128]{1,0:T(8,128)S(1)}, u32[]{:S(2)}, u32[]{:S(2)}) collective-permute-start(f32[512,128]{1,0:T(8,128)S(1)} %pad_maximum_fusion.2), channel_id=1, source_target_pairs={{0,4},{4,0},{8,12},{12,8},{16,20},{20,16},{24,28},{28,24},{1,5},{5... | collective-permute-start | bytes 786440 | tf_op jit(solution)/shard_map/step_1/ppermute | solution.py:22
  4.2 5.1 %collective-permute-start = (f32[512,128]{1,0:T(8,128)}, f32[512,128]{1,0:T(8,128)S(1)}, u32[]{:S(2)}, u32[]{:S(2)}) collective-permute-start(f32[512,128]{1,0:T(8,128)} %refs_0_.1), channel_id=1, source_target_pairs={{0,3},{1,0},{2,1},{3,2},{4,7},{5,4},{6,5},{7,6},{8,11},{9,8},{10,9... | collective-permute-start | bytes 786440 | tf_op jit(solution)/shard_map/step_1/ppermute | solution.py:17
  9.3 2.5 %collective-permute-start.2 = (f32[512,128]{1,0:T(8,128)}, f32[512,128]{1,0:T(8,128)S(1)}, u32[]{:S(2)}, u32[]{:S(2)}) collective-permute-start(f32[512,128]{1,0:T(8,128)} %refs_0_.1), channel_id=1, source_target_pairs={{0,192},{32,224},{64,0},{96,32},{128,64},{160,96},{192,128},{224,1... | collective-permute-start | bytes 786440 | tf_op jit(solution)/shard_map/step_1/ppermute | solution.py:17
  11.8 1.0 pad_maximum_fusion.1
  12.8 1.8 collective-permute-done.refs_8_
  14.6 11.6 %collective-permute-done.1.refs_12_ = f32[512,128]{1,0:T(8,128)S(1)} collective-permute-done((f32[512,128]{1,0:T(8,128)}, f32[512,128]{1,0:T(8,128)S(1)}, u32[]{:S(2)}, u32[]{:S(2)}) %collective-permute-start.1) | collective-permute-done | bytes 262176 | tf_op jit(solution)/shard_map/step_1/ppermute | solution.py:17
  26.3 1.5 broadcast_in_dim.41
  27.8 4.3 %all-to-all-start = ((f32[4,1024,128]{2,1,0:T(8,128)}), f32[4,1024,128]{2,1,0:T(8,128)S(1)}, u32[]{:S(2)}, u32[]{:S(2)}) async-start(f32[4,1024,128]{2,1,0:T(8,128)} %broadcast_in_dim.41), calls=%async_computation | async-start | bytes 4194304 | tf_op jit(solution)/shard_map/step_2/all_to_all | solution.py:239
  32.2 1.2 collective-permute-start.5
  33.4 1.3 collective-permute-start.6
  34.7 2.5 %collective-permute-start.7 = (f32[512,128]{1,0:T(8,128)S(1)}, f32[512,128]{1,0:T(8,128)S(1)}, u32[]{:S(2)}, u32[]{:S(2)}) collective-permute-start(f32[512,128]{1,0:T(8,128)S(1)} %collective-permute-done.refs_8_), channel_id=1, source_target_pairs={{0,192},{32,224},{64,0},{96,32},{128,64},{160,96},{192,128},{224,1... | collective-permute-start | bytes 786440 | tf_op jit(solution)/shard_map/step_2/ppermute | solution.py:17
  37.2 2.7 %collective-permute-start.9 = (f32[512,128]{1,0:T(8,128)S(1)}, f32[512,128]{1,0:T(8,128)S(1)}, u32[]{:S(2)}, u32[]{:S(2)}) collective-permute-start(f32[512,128]{1,0:T(8,128)S(1)} %collective-permute-done.1.refs_12_), channel_id=1, source_target_pairs={{0,192},{32,224},{64,0},{96,32},{128,64},{160,96},{192,128},{224,1... | collective-permute-start | bytes 786440 | tf_op jit(solution)/shard_map/step_2/ppermute | solution.py:17
  39.9 0.8 collective-permute-done.6
  40.7 2.6 %collective-permute-start.11 = (f32[512,128]{1,0:T(8,128)S(1)}, f32[512,128]{1,0:T(8,128)}, u32[]{:S(2)}, u32[]{:S(2)}) collective-permute-start(f32[512,128]{1,0:T(8,128)S(1)} %constant_dynamic-update-slice_fusion.refs_4_), channel_id=1, source_target_pairs={{0,192},{32,224},{64,0},{96,32},{128,64},{160,96},{192,128},{224,1... | collective-permute-start | bytes 786440 | tf_op jit(solution)/shard_map/step_3/ppermute | solution.py:17
  43.9 1.2 collective-permute-start.13
  45.1 0.9 collective-permute-done.9.refs_13_
  46.0 3.4 %collective-permute-start.14 = (f32[512,128]{1,0:T(8,128)S(1)}, f32[512,128]{1,0:T(8,128)}, u32[]{:S(2)}, u32[]{:S(2)}) collective-permute-start(f32[512,128]{1,0:T(8,128)S(1)} %collective-permute-done.2.refs_1_), channel_id=1, source_target_pairs={{0,192},{32,224},{64,0},{96,32},{128,64},{160,96},{192,128},{224,1... | collective-permute-start | bytes 786440 | tf_op jit(solution)/shard_map/step_3/ppermute | solution.py:17
  49.6 13.6 %collective-permute-start.16 = (f32[128,128]{0,1:T(8,128)S(1)}, f32[128,128]{0,1:T(8,128)S(1)}, u32[]{:S(2)}, u32[]{:S(2)}) collective-permute-start(f32[128,128]{0,1:T(8,128)S(1)} %copy.16), channel_id=1, source_target_pairs={{0,0},{1,4},{2,8},{3,12},{4,1},{5,5},{6,9},{7,13},{8,2},{9,6},{10,... | collective-permute-start | bytes 196616 | tf_op jit(solution)/shard_map/step_3/ppermute | solution.py:255
  63.3 1.8 collective-permute-done.16
  65.1 7.6 %collective-permute-start.15 = (f32[384,128]{0,1:T(8,128)S(1)}, f32[384,128]{0,1:T(8,128)}, u32[]{:S(2)}, u32[]{:S(2)}) collective-permute-start(f32[384,128]{0,1:T(8,128)S(1)} %copy.15), channel_id=1, source_target_pairs={{0,0},{1,1},{2,4},{3,5},{4,2},{5,3},{6,6},{7,7},{8,32},{9,33},{10,... | collective-permute-start | bytes 589832 | tf_op jit(solution)/shard_map/step_3/ppermute | solution.py:254
  72.8 3.6 %collective-permute-done.15 = f32[384,128]{0,1:T(8,128)} collective-permute-done((f32[384,128]{0,1:T(8,128)S(1)}, f32[384,128]{0,1:T(8,128)}, u32[]{:S(2)}, u32[]{:S(2)}) %collective-permute-start.15) | collective-permute-done | bytes 196640 | tf_op jit(solution)/shard_map/step_3/ppermute | solution.py:254
  77.1 2.8 %collective-permute-start.21 = (f32[512,128]{1,0:T(8,128)}, f32[512,128]{1,0:T(8,128)}, u32[]{:S(2)}, u32[]{:S(2)}) collective-permute-start(f32[512,128]{1,0:T(8,128)} %collective-permute-done.10.refs_14_), channel_id=1, source_target_pairs={{0,64},{32,96},{64,128},{96,160},{128,192},{160,224},{192,0},{224,... | collective-permute-start | bytes 786440 | tf_op jit(solution)/shard_map/step_4/ppermute | solution.py:17
  80.5 7.6 %collective-permute-start.18 = (f32[128,384]{1,0:T(8,128)}, f32[128,384]{1,0:T(8,128)S(1)}, u32[]{:S(2)}, u32[]{:S(2)}) collective-permute-start(f32[128,384]{1,0:T(8,128)} %bitcast.16), channel_id=1, source_target_pairs={{0,3},{1,0},{2,1},{3,2},{4,7},{5,4},{6,5},{7,6},{8,11},{9,8},{10,9... | collective-permute-start | bytes 589832 | tf_op jit(solution)/shard_map/step_4/ppermute | solution.py:17
  88.6 7.4 %collective-permute-done.18 = f32[128,384]{1,0:T(8,128)S(1)} collective-permute-done((f32[128,384]{1,0:T(8,128)}, f32[128,384]{1,0:T(8,128)S(1)}, u32[]{:S(2)}, u32[]{:S(2)}) %collective-permute-start.18) | collective-permute-done | bytes 196640 | tf_op jit(solution)/shard_map/step_4/ppermute | solution.py:17
  96.0 3.0 %collective-permute-done.19 = f32[128,384]{1,0:T(8,128)S(1)} collective-permute-done((f32[128,384]{1,0:T(8,128)}, f32[128,384]{1,0:T(8,128)S(1)}, u32[]{:S(2)}, u32[]{:S(2)}) %collective-permute-start.19) | collective-permute-done | bytes 196640 | tf_op jit(solution)/shard_map/step_4/ppermute | solution.py:17
  99.1 0.7 copy-done.20
  99.8 6.6 %border_middle.1 = (f32[512,128]{1,0:T(8,128)}, f32[512,128]{1,0:T(8,128)}) custom-call(s32[16]{0:T(128)} %compare_select_fusion.8.places_ref, f32[512,128]{1,0:T(8,128)} %refs_0_.1, f32[512,128]{1,0:T(8,128)} %copy-done.14, f32[512,128]{1,0:T(8,128)} %copy-done.15, f32[512,128]{1,0:T(8,128)} %collective-permute-done.14.refs_3_, f32[512,128]{1,0:T(8,128)} %copy-done.12, ...), custom_call_target="tpu_custom_call" | custom-call | flops 1610612736 | bytes 33554432 | tf_op jit(solution)/shard_map/border_middle/pallas_call | solution.py:90
  106.4 2.1 collective-permute-start.22
  108.8 2.2 %collective-permute-start.24 = (f32[64,384]{1,0:T(8,128)S(1)}, f32[64,384]{1,0:T(8,128)S(1)}, u32[]{:S(2)}, u32[]{:S(2)}) collective-permute-start(f32[64,384]{1,0:T(8,128)S(1)} %slice.33), channel_id=1, source_target_pairs={{0,1},{1,2},{2,3},{3,0},{4,5},{5,6},{6,7},{7,4},{8,9},{9,10},{10,1... | collective-permute-start | bytes 294920 | tf_op jit(solution)/shard_map/panel_columns/ppermute | solution.py:17
  111.0 1.0 add.335
  112.0 1.9 collective-permute-done.23
  113.9 1.2 collective-permute-done.24
  115.1 1.5 broadcast_in_dim.42
  116.6 5.9 %all-to-all-start.1 = ((f32[8,512,128]{2,1,0:T(8,128)}), f32[8,512,128]{2,1,0:T(8,128)}, u32[]{:S(2)}, u32[]{:S(2)}) async-start(f32[8,512,128]{2,1,0:T(8,128)} %broadcast_in_dim.42), calls=%async_computation.1 | async-start | bytes 4194304 | tf_op jit(solution)/shard_map/border_middle/all_to_all | solution.py:160
  122.5 1.0 pad_maximum_fusion.refs_0_
  123.5 1.4 collective-permute-start.25
  125.8 1.4 collective-permute-start.26
  127.2 14.2 %collective-permute-done.25.refs_1_ = f32[4,128,384]{2,1,0:T(8,128)S(1)} collective-permute-done((f32[4,128,384]{2,1,0:T(8,128)S(1)}, f32[4,128,384]{2,1,0:T(8,128)S(1)}, u32[]{:S(2)}, u32[]{:S(2)}) %collective-permute-start.25) | collective-permute-done | bytes 786464 | tf_op jit(solution)/shard_map/panel_columns/ppermute | solution.py:22
  141.4 2.1 collective-permute-start.27
  143.9 1.8 collective-permute-done.27.refs_3_
  145.6 2.7 %all-to-all-done.1 = f32[8,512,128]{2,1,0:T(8,128)} async-done(((f32[8,512,128]{2,1,0:T(8,128)}), f32[8,512,128]{2,1,0:T(8,128)}, u32[]{:S(2)}, u32[]{:S(2)}) %all-to-all-start.1) | async-done | bytes 2097184 | tf_op jit(solution)/shard_map/border_middle/all_to_all | solution.py:160
  148.3 4.8 %inverse_middle.1 = (f32[384,128]{1,0:T(8,128)}, f32[256,128]{1,0:T(8,128)}) custom-call(s32[24]{0:T(128)} %copy-done.25, s32[16]{0:T(128)} %add.308.spots_ref, s32[1]{0:T(128)} %bitcast.5.where_ref, f32[4096,128]{1,0:T(8,128)} %bitcast.17.full_ref, f32[4,128,384]{2,1,0:T(8,128)} %copy-done.3, f32[4,128,384]{2,1,0:T(8,128)} %copy-done.8, ...), custom_call_target="tpu_custom_call" | custom-call | tf_op jit(solution)/shard_map/inverse_middle/pallas_call | solution.py:144
  153.1 0.9 pad_maximum_fusion.5
  154.0 2.0 collective-permute-start.30
  155.9 1.7 collective-permute-start.29
  157.6 10.0 %collective-permute-done.29 = f32[384,128]{1,0:T(8,128)S(1)} collective-permute-done((f32[384,128]{1,0:T(8,128)S(1)}, f32[384,128]{1,0:T(8,128)S(1)}, u32[]{:S(2)}, u32[]{:S(2)}) %collective-permute-start.29) | collective-permute-done | bytes 196640 | tf_op jit(solution)/shard_map/parent_rows/ppermute | solution.py:17
  167.7 2.3 %collective-permute-start.32 = (f32[384,128]{1,0:T(8,128)S(1)}, f32[384,128]{1,0:T(8,128)S(1)}, u32[]{:S(2)}, u32[]{:S(2)}) collective-permute-start(f32[384,128]{1,0:T(8,128)S(1)} %collective-permute-done.29), channel_id=1, source_target_pairs={{0,3},{1,0},{2,1},{3,2},{4,7},{5,4},{6,5},{7,6},{8,11},{9,8},{10,9... | collective-permute-start | bytes 589832 | tf_op jit(solution)/shard_map/parent_rows/ppermute | solution.py:17
  170.1 1.5 collective-permute-start.31
  172.4 5.3 %collective-permute-done.32.refs_4_ = f32[384,128]{1,0:T(8,128)S(1)} collective-permute-done((f32[384,128]{1,0:T(8,128)S(1)}, f32[384,128]{1,0:T(8,128)S(1)}, u32[]{:S(2)}, u32[]{:S(2)}) %collective-permute-start.32) | collective-permute-done | bytes 196640 | tf_op jit(solution)/shard_map/parent_rows/ppermute | solution.py:17
  178.3 0.7 collective-permute-done.28.refs_1_
  179.1 4.3 %collective-permute-done.33.refs_5_ = f32[256,128]{1,0:T(8,128)S(1)} collective-permute-done((f32[256,128]{1,0:T(8,128)S(1)}, f32[256,128]{1,0:T(8,128)S(1)}, u32[]{:S(2)}, u32[]{:S(2)}) %collective-permute-start.33) | collective-permute-done | bytes 131104 | tf_op jit(solution)/shard_map/parent_rows/ppermute | solution.py:22
  184.1 3.3 %border_lower.1 = (f32[256,128]{1,0:T(8,128)}, f32[256,128]{1,0:T(8,128)}) custom-call(s32[8]{0:T(128)} %compare_select_fusion.12.places_ref, f32[256,128]{1,0:T(8,128)} %get-tuple-element.40.refs_0_, f32[256,128]{1,0:T(8,128)} %copy-done.23, f32[512,128]{1,0:T(8,128)} %copy-done.5, f32[512,128]{1,0:T(8,128)} %copy-done.21, f32[384,128]{1,0:T(8,128)} %copy-done.7, ...), custom_call_target="tpu_custom_call" | custom-call | flops 402653184 | bytes 8388608 | tf_op jit(solution)/shard_map/border_lower/pallas_call | solution.py:90
  187.4 2.1 collective-permute-start.34
  189.5 1.2 collective-permute-done.34
  190.6 0.9 add.354
  191.6 1.1 broadcast_in_dim.46
  192.7 4.2 %all-to-all-start.2 = ((f32[8,256,128]{2,1,0:T(8,128)}), f32[8,256,128]{2,1,0:T(8,128)S(1)}, u32[]{:S(2)}, u32[]{:S(2)}) async-start(f32[8,256,128]{2,1,0:T(8,128)} %broadcast_in_dim.46), calls=%async_computation.2 | async-start | bytes 2097152 | tf_op jit(solution)/shard_map/border_lower/all_to_all | solution.py:160
  196.9 0.8 slice_bitcast_fusion.1
  197.7 0.7 collective-permute-start.35
  198.5 0.7 add.340.spots_ref
  199.6 12.4 %all-to-all-done.2 = f32[8,256,128]{2,1,0:T(8,128)S(1)} async-done(((f32[8,256,128]{2,1,0:T(8,128)}), f32[8,256,128]{2,1,0:T(8,128)S(1)}, u32[]{:S(2)}, u32[]{:S(2)}) %all-to-all-start.2) | async-done | bytes 1048608 | tf_op jit(solution)/shard_map/border_lower/all_to_all | solution.py:160
  212.0 1.0 copy-done.2
  213.1 2.4 %inverse_lower.1 = (f32[128,128]{1,0:T(8,128)}, f32[128,128]{1,0:T(8,128)}) custom-call(s32[8]{0:T(128)} %copy-done.26, s32[8]{0:T(128)} %add.340.spots_ref, s32[1]{0:T(128)} %bitcast.5.where_ref, f32[2048,128]{1,0:T(8,128)} %bitcast.43, f32[4,128,128]{2,1,0:T(8,128)} %copy-done.6, f32[4,128,128]{2,1,0:T(8,128)} %copy-done.22, f32[128,128]{1,0:T(8,128)} %refs_2_.1), custom_call_target="tpu_custom_call" | custom-call | tf_op jit(solution)/shard_map/inverse_lower/pallas_call | solution.py:144
  (129 shorter events, 6.9 us)
Async XLA Ops:
  0.6 143.1 %copy-start = (s32[4,8]{1,0:T(4,128)S(1)}, s32[4,8]{1,0:T(4,128)}, u32[]{:S(2)}) copy-start(s32[4,8]{1,0:T(4,128)} %param.13) | copy-start | bytes 388
  1.6 10.2 %collective-permute-start.4 = (f32[512,128]{1,0:T(8,128)S(1)}, f32[512,128]{1,0:T(8,128)S(1)}, u32[]{:S(2)}, u32[]{:S(2)}) collective-permute-start(f32[512,128]{1,0:T(8,128)S(1)} %pad_maximum_fusion.2), channel_id=1, source_target_pairs={{0,4},{4,0},{8,12},{12,8},{16,20},{20,16},{24,28},{28,24},{1,5},{5... | collective-permute-start | bytes 786440 | tf_op jit(solution)/shard_map/step_1/ppermute | solution.py:22
  4.2 10.5 %collective-permute-start = (f32[512,128]{1,0:T(8,128)}, f32[512,128]{1,0:T(8,128)S(1)}, u32[]{:S(2)}, u32[]{:S(2)}) collective-permute-start(f32[512,128]{1,0:T(8,128)} %refs_0_.1), channel_id=1, source_target_pairs={{0,3},{1,0},{2,1},{3,2},{4,7},{5,4},{6,5},{7,6},{8,11},{9,8},{10,9... | collective-permute-start | bytes 786440 | tf_op jit(solution)/shard_map/step_1/ppermute | solution.py:17
  9.3 16.9 %collective-permute-start.1 = (f32[512,128]{1,0:T(8,128)}, f32[512,128]{1,0:T(8,128)S(1)}, u32[]{:S(2)}, u32[]{:S(2)}) collective-permute-start(f32[512,128]{1,0:T(8,128)} %refs_0_.1), channel_id=1, source_target_pairs={{0,1},{1,2},{2,3},{3,0},{4,5},{5,6},{6,7},{7,4},{8,9},{9,10},{10,1... | collective-permute-start | bytes 786440 | tf_op jit(solution)/shard_map/step_1/ppermute | solution.py:17
  9.3 16.9 %collective-permute-start.2 = (f32[512,128]{1,0:T(8,128)}, f32[512,128]{1,0:T(8,128)S(1)}, u32[]{:S(2)}, u32[]{:S(2)}) collective-permute-start(f32[512,128]{1,0:T(8,128)} %refs_0_.1), channel_id=1, source_target_pairs={{0,192},{32,224},{64,0},{96,32},{128,64},{160,96},{192,128},{224,1... | collective-permute-start | bytes 786440 | tf_op jit(solution)/shard_map/step_1/ppermute | solution.py:17
  11.8 14.5 %collective-permute-start.3 = (f32[512,128]{1,0:T(8,128)}, f32[512,128]{1,0:T(8,128)S(1)}, u32[]{:S(2)}, u32[]{:S(2)}) collective-permute-start(f32[512,128]{1,0:T(8,128)} %refs_0_.1), channel_id=1, source_target_pairs={{0,64},{32,96},{64,128},{96,160},{128,192},{160,224},{192,0},{224,... | collective-permute-start | bytes 786440 | tf_op jit(solution)/shard_map/step_1/ppermute | solution.py:17
  14.6 22.5 %copy-start.10 = (f32[512,128]{1,0:T(8,128)}, f32[512,128]{1,0:T(8,128)S(1)}, u32[]{:S(2)}) copy-start(f32[512,128]{1,0:T(8,128)S(1)} %collective-permute-done.refs_8_) | copy-start | bytes 786436
  26.3 13.6 %copy-start.11 = (f32[512,128]{1,0:T(8,128)}, f32[512,128]{1,0:T(8,128)S(1)}, u32[]{:S(2)}) copy-start(f32[512,128]{1,0:T(8,128)S(1)} %collective-permute-done.1.refs_12_) | copy-start | bytes 786436
  26.3 19.8 %copy-start.14 = (f32[512,128]{1,0:T(8,128)}, f32[512,128]{1,0:T(8,128)S(1)}, u32[]{:S(2)}) copy-start(f32[512,128]{1,0:T(8,128)S(1)} %collective-permute-done.2.refs_1_) | copy-start | bytes 786436
  26.3 1.6 copy-start.15
  27.8 21.6 %copy-start.13 = (f32[128,128]{1,0:T(8,128)S(1)}, f32[128,128]{1,0:T(8,128)}, u32[]{:S(2)}) copy-start(f32[128,128]{1,0:T(8,128)} %param.10) | copy-start | bytes 196612
  27.8 35.3 %copy-start.4 = (f32[384,128]{1,0:T(8,128)S(1)}, f32[384,128]{1,0:T(8,128)}, u32[]{:S(2)}) copy-start(f32[384,128]{1,0:T(8,128)} %param.8) | copy-start | bytes 589828
  27.8 48.9 %copy-start.27 = (s32[2,24]{1,0:T(2,128)S(1)}, s32[2,24]{1,0:T(2,128)}, u32[]{:S(2)}) copy-start(s32[2,24]{1,0:T(2,128)} %param.12) | copy-start | bytes 580
  27.8 48.6 %all-to-all-start = ((f32[4,1024,128]{2,1,0:T(8,128)}), f32[4,1024,128]{2,1,0:T(8,128)S(1)}, u32[]{:S(2)}, u32[]{:S(2)}) async-start(f32[4,1024,128]{2,1,0:T(8,128)} %broadcast_in_dim.41), calls=%async_computation | async-start | bytes 4194304 | tf_op jit(solution)/shard_map/step_2/all_to_all | solution.py:239
  32.2 7.7 %collective-permute-start.5 = (f32[256,128]{1,0:T(8,128)S(1)}, f32[256,128]{1,0:T(8,128)S(1)}, u32[]{:S(2)}, u32[]{:S(2)}) collective-permute-start(f32[256,128]{1,0:T(8,128)S(1)} %slice.30), channel_id=1, source_target_pairs={{0,3},{1,0},{2,1},{3,2},{4,7},{5,4},{6,5},{7,6},{8,11},{9,8},{10,9... | collective-permute-start | bytes 393224 | tf_op jit(solution)/shard_map/step_2/ppermute | solution.py:17
  33.4 7.3 %collective-permute-start.6 = (f32[256,128]{1,0:T(8,128)S(1)}, f32[256,128]{1,0:T(8,128)S(1)}, u32[]{:S(2)}, u32[]{:S(2)}) collective-permute-start(f32[256,128]{1,0:T(8,128)S(1)} %slice.31), channel_id=1, source_target_pairs={{0,1},{1,2},{2,3},{3,0},{4,5},{5,6},{6,7},{7,4},{8,9},{9,10},{10,1... | collective-permute-start | bytes 393224 | tf_op jit(solution)/shard_map/step_2/ppermute | solution.py:17
  34.7 8.6 %collective-permute-start.7 = (f32[512,128]{1,0:T(8,128)S(1)}, f32[512,128]{1,0:T(8,128)S(1)}, u32[]{:S(2)}, u32[]{:S(2)}) collective-permute-start(f32[512,128]{1,0:T(8,128)S(1)} %collective-permute-done.refs_8_), channel_id=1, source_target_pairs={{0,192},{32,224},{64,0},{96,32},{128,64},{160,96},{192,128},{224,1... | collective-permute-start | bytes 786440 | tf_op jit(solution)/shard_map/step_2/ppermute | solution.py:17
  37.2 6.7 %collective-permute-start.8 = (f32[512,128]{1,0:T(8,128)S(1)}, f32[512,128]{1,0:T(8,128)S(1)}, u32[]{:S(2)}, u32[]{:S(2)}) collective-permute-start(f32[512,128]{1,0:T(8,128)S(1)} %collective-permute-done.refs_8_), channel_id=1, source_target_pairs={{0,64},{32,96},{64,128},{96,160},{128,192},{160,224},{192,0},{224,... | collective-permute-start | bytes 786440 | tf_op jit(solution)/shard_map/step_2/ppermute | solution.py:17
  37.2 8.8 %collective-permute-start.9 = (f32[512,128]{1,0:T(8,128)S(1)}, f32[512,128]{1,0:T(8,128)S(1)}, u32[]{:S(2)}, u32[]{:S(2)}) collective-permute-start(f32[512,128]{1,0:T(8,128)S(1)} %collective-permute-done.1.refs_12_), channel_id=1, source_target_pairs={{0,192},{32,224},{64,0},{96,32},{128,64},{160,96},{192,128},{224,1... | collective-permute-start | bytes 786440 | tf_op jit(solution)/shard_map/step_2/ppermute | solution.py:17
  39.9 9.6 %collective-permute-start.10 = (f32[512,128]{1,0:T(8,128)S(1)}, f32[512,128]{1,0:T(8,128)}, u32[]{:S(2)}, u32[]{:S(2)}) collective-permute-start(f32[512,128]{1,0:T(8,128)S(1)} %collective-permute-done.1.refs_12_), channel_id=1, source_target_pairs={{0,64},{32,96},{64,128},{96,160},{128,192},{160,224},{192,0},{224,... | collective-permute-start | bytes 786440 | tf_op jit(solution)/shard_map/step_2/ppermute | solution.py:17
  40.7 58.3 %copy-start.12 = (f32[512,128]{1,0:T(8,128)}, f32[512,128]{1,0:T(8,128)S(1)}, u32[]{:S(2)}) copy-start(f32[512,128]{1,0:T(8,128)S(1)} %constant_dynamic-update-slice_fusion.refs_4_) | copy-start | bytes 786436
  40.7 32.0 %collective-permute-start.11 = (f32[512,128]{1,0:T(8,128)S(1)}, f32[512,128]{1,0:T(8,128)}, u32[]{:S(2)}, u32[]{:S(2)}) collective-permute-start(f32[512,128]{1,0:T(8,128)S(1)} %constant_dynamic-update-slice_fusion.refs_4_), channel_id=1, source_target_pairs={{0,192},{32,224},{64,0},{96,32},{128,64},{160,96},{192,128},{224,1... | collective-permute-start | bytes 786440 | tf_op jit(solution)/shard_map/step_3/ppermute | solution.py:17
  43.3 6.1 %copy-start.16 = (f32[512,128]{1,0:T(8,128)}, f32[512,128]{1,0:T(8,128)S(1)}, u32[]{:S(2)}) copy-start(f32[512,128]{1,0:T(8,128)S(1)} %collective-permute-done.7.refs_9_) | copy-start | bytes 786436
  43.3 29.4 %collective-permute-start.12 = (f32[512,128]{1,0:T(8,128)S(1)}, f32[512,128]{1,0:T(8,128)}, u32[]{:S(2)}, u32[]{:S(2)}) collective-permute-start(f32[512,128]{1,0:T(8,128)S(1)} %constant_dynamic-update-slice_fusion.refs_4_), channel_id=1, source_target_pairs={{0,64},{32,96},{64,128},{96,160},{128,192},{160,224},{192,0},{224,... | collective-permute-start | bytes 786440 | tf_op jit(solution)/shard_map/step_3/ppermute | solution.py:17
  43.9 5.5 %copy-start.17 = (f32[512,128]{1,0:T(8,128)}, f32[512,128]{1,0:T(8,128)S(1)}, u32[]{:S(2)}) copy-start(f32[512,128]{1,0:T(8,128)S(1)} %collective-permute-done.8.refs_10_) | copy-start | bytes 786436
  43.9 28.8 %collective-permute-start.13 = (f32[512,128]{1,0:T(8,128)S(1)}, f32[512,128]{1,0:T(8,128)S(1)}, u32[]{:S(2)}, u32[]{:S(2)}) collective-permute-start(f32[512,128]{1,0:T(8,128)S(1)} %constant_dynamic-update-slice_fusion.refs_4_), channel_id=1, source_target_pairs={{0,128},{32,160},{64,192},{96,224},{128,0},{160,32},{192,64},{224,... | collective-permute-start | bytes 786440 | tf_op jit(solution)/shard_map/step_3/ppermute | solution.py:17
  46.0 3.4 %copy-start.18 = (f32[512,128]{1,0:T(8,128)}, f32[512,128]{1,0:T(8,128)S(1)}, u32[]{:S(2)}) copy-start(f32[512,128]{1,0:T(8,128)S(1)} %collective-permute-done.9.refs_13_) | copy-start | bytes 786436
  46.0 26.7 %collective-permute-start.14 = (f32[512,128]{1,0:T(8,128)S(1)}, f32[512,128]{1,0:T(8,128)}, u32[]{:S(2)}, u32[]{:S(2)}) collective-permute-start(f32[512,128]{1,0:T(8,128)S(1)} %collective-permute-done.2.refs_1_), channel_id=1, source_target_pairs={{0,192},{32,224},{64,0},{96,32},{128,64},{160,96},{192,128},{224,1... | collective-permute-start | bytes 786440 | tf_op jit(solution)/shard_map/step_3/ppermute | solution.py:17
  49.6 15.5 %collective-permute-start.16 = (f32[128,128]{0,1:T(8,128)S(1)}, f32[128,128]{0,1:T(8,128)S(1)}, u32[]{:S(2)}, u32[]{:S(2)}) collective-permute-start(f32[128,128]{0,1:T(8,128)S(1)} %copy.16), channel_id=1, source_target_pairs={{0,0},{1,4},{2,8},{3,12},{4,1},{5,5},{6,9},{7,13},{8,2},{9,6},{10,... | collective-permute-start | bytes 196616 | tf_op jit(solution)/shard_map/step_3/ppermute | solution.py:255
  65.1 11.3 %collective-permute-start.15 = (f32[384,128]{0,1:T(8,128)S(1)}, f32[384,128]{0,1:T(8,128)}, u32[]{:S(2)}, u32[]{:S(2)}) collective-permute-start(f32[384,128]{0,1:T(8,128)S(1)} %copy.15), channel_id=1, source_target_pairs={{0,0},{1,1},{2,4},{3,5},{4,2},{5,3},{6,6},{7,7},{8,32},{9,33},{10,... | collective-permute-start | bytes 589832 | tf_op jit(solution)/shard_map/step_3/ppermute | solution.py:254
  72.8 26.3 %copy-start.19 = (f32[512,128]{1,0:T(8,128)}, f32[512,128]{1,0:T(8,128)S(1)}, u32[]{:S(2)}) copy-start(f32[512,128]{1,0:T(8,128)S(1)} %collective-permute-done.13.refs_7_) | copy-start | bytes 786436
  76.4 22.7 %copy-start.1 = (f32[4,1024,128]{2,1,0:T(8,128)}, f32[4,1024,128]{2,1,0:T(8,128)S(1)}, u32[]{:S(2)}) copy-start(f32[4,1024,128]{2,1,0:T(8,128)S(1)} %all-to-all-done) | copy-start | bytes 6291460
  76.4 22.6 %collective-permute-start.17 = (f32[4096,128]{1,0:T(8,128)S(1)}, f32[4096,128]{1,0:T(8,128)}, u32[]{:S(2)}, u32[]{:S(2)}) collective-permute-start(f32[4096,128]{1,0:T(8,128)S(1)} %bitcast.40), channel_id=1, source_target_pairs={{0,32},{32,0},{64,96},{96,64},{128,160},{160,128},{192,224},{224,1... | collective-permute-start | bytes 6291464 | tf_op jit(solution)/shard_map/step_4/ppermute | solution.py:22
  76.8 29.6 %copy-start.25 = (s32[24]{0:T(128)}, s32[24]{0:T(128)S(1)}, u32[]{:S(2)}) copy-start(s32[24]{0:T(128)S(1)} %dynamic-slice_bitcast_fusion.1.tiles_ref) | copy-start | bytes 292
  76.9 22.1 %collective-permute-start.20 = (f32[512,128]{1,0:T(8,128)}, f32[512,128]{1,0:T(8,128)S(1)}, u32[]{:S(2)}, u32[]{:S(2)}) collective-permute-start(f32[512,128]{1,0:T(8,128)} %copy-done.16), channel_id=1, source_target_pairs={{0,192},{32,224},{64,0},{96,32},{128,64},{160,96},{192,128},{224,1... | collective-permute-start | bytes 786440 | tf_op jit(solution)/shard_map/step_4/ppermute | solution.py:17
  77.1 22.0 %collective-permute-start.21 = (f32[512,128]{1,0:T(8,128)}, f32[512,128]{1,0:T(8,128)}, u32[]{:S(2)}, u32[]{:S(2)}) collective-permute-start(f32[512,128]{1,0:T(8,128)} %collective-permute-done.10.refs_14_), channel_id=1, source_target_pairs={{0,64},{32,96},{64,128},{96,160},{128,192},{160,224},{192,0},{224,... | collective-permute-start | bytes 786440 | tf_op jit(solution)/shard_map/step_4/ppermute | solution.py:17
  80.5 15.5 %collective-permute-start.18 = (f32[128,384]{1,0:T(8,128)}, f32[128,384]{1,0:T(8,128)S(1)}, u32[]{:S(2)}, u32[]{:S(2)}) collective-permute-start(f32[128,384]{1,0:T(8,128)} %bitcast.16), channel_id=1, source_target_pairs={{0,3},{1,0},{2,1},{3,2},{4,7},{5,4},{6,5},{7,6},{8,11},{9,8},{10,9... | collective-permute-start | bytes 589832 | tf_op jit(solution)/shard_map/step_4/ppermute | solution.py:17
  88.0 11.0 %collective-permute-start.19 = (f32[128,384]{1,0:T(8,128)}, f32[128,384]{1,0:T(8,128)S(1)}, u32[]{:S(2)}, u32[]{:S(2)}) collective-permute-start(f32[128,384]{1,0:T(8,128)} %bitcast.16), channel_id=1, source_target_pairs={{0,1},{1,2},{2,3},{3,0},{4,5},{5,6},{6,7},{7,4},{8,9},{9,10},{10,1... | collective-permute-start | bytes 589832 | tf_op jit(solution)/shard_map/step_4/ppermute | solution.py:17
  106.4 4.7 %collective-permute-start.22 = (f32[512,128]{1,0:T(8,128)}, f32[512,128]{1,0:T(8,128)S(1)}, u32[]{:S(2)}, u32[]{:S(2)}) collective-permute-start(f32[512,128]{1,0:T(8,128)} %get-tuple-element.69), channel_id=1, source_target_pairs={{0,32},{32,0},{64,96},{96,64},{128,160},{160,128},{192,224},{224,1... | collective-permute-start | bytes 786440 | tf_op jit(solution)/shard_map/border_middle/ppermute | solution.py:22
  108.5 5.4 %collective-permute-start.23 = (f32[64,384]{1,0:T(8,128)S(1)}, f32[64,384]{1,0:T(8,128)S(1)}, u32[]{:S(2)}, u32[]{:S(2)}) collective-permute-start(f32[64,384]{1,0:T(8,128)S(1)} %slice.32), channel_id=1, source_target_pairs={{0,3},{1,0},{2,1},{3,2},{4,7},{5,4},{6,5},{7,6},{8,11},{9,8},{10,9... | collective-permute-start | bytes 294920 | tf_op jit(solution)/shard_map/panel_columns/ppermute | solution.py:17
  108.8 6.3 %collective-permute-start.24 = (f32[64,384]{1,0:T(8,128)S(1)}, f32[64,384]{1,0:T(8,128)S(1)}, u32[]{:S(2)}, u32[]{:S(2)}) collective-permute-start(f32[64,384]{1,0:T(8,128)S(1)} %slice.33), channel_id=1, source_target_pairs={{0,1},{1,2},{2,3},{3,0},{4,5},{5,6},{6,7},{7,4},{8,9},{9,10},{10,1... | collective-permute-start | bytes 294920 | tf_op jit(solution)/shard_map/panel_columns/ppermute | solution.py:17
  116.6 31.7 %all-to-all-start.1 = ((f32[8,512,128]{2,1,0:T(8,128)}), f32[8,512,128]{2,1,0:T(8,128)}, u32[]{:S(2)}, u32[]{:S(2)}) async-start(f32[8,512,128]{2,1,0:T(8,128)} %broadcast_in_dim.42), calls=%async_computation.1 | async-start | bytes 4194304 | tf_op jit(solution)/shard_map/border_middle/all_to_all | solution.py:160
  123.5 24.8 %copy-start.3 = (f32[4,128,384]{2,1,0:T(8,128)}, f32[4,128,384]{2,1,0:T(8,128)S(1)}, u32[]{:S(2)}) copy-start(f32[4,128,384]{2,1,0:T(8,128)S(1)} %pad_maximum_fusion.refs_0_) | copy-start | bytes 2359300
  123.5 17.9 %collective-permute-start.25 = (f32[4,128,384]{2,1,0:T(8,128)S(1)}, f32[4,128,384]{2,1,0:T(8,128)S(1)}, u32[]{:S(2)}, u32[]{:S(2)}) collective-permute-start(f32[4,128,384]{2,1,0:T(8,128)S(1)} %pad_maximum_fusion.refs_0_), channel_id=1, source_target_pairs={{0,64},{32,96},{64,0},{96,32},{128,192},{160,224},{192,128},{224,1... | collective-permute-start | bytes 2359304 | tf_op jit(solution)/shard_map/panel_columns/ppermute | solution.py:22
  125.8 18.1 %collective-permute-start.26 = (f32[4,128,384]{2,1,0:T(8,128)S(1)}, f32[4,128,384]{2,1,0:T(8,128)S(1)}, u32[]{:S(2)}, u32[]{:S(2)}) collective-permute-start(f32[4,128,384]{2,1,0:T(8,128)S(1)} %pad_maximum_fusion.refs_0_), channel_id=1, source_target_pairs={{0,32},{32,0},{64,96},{96,64},{128,160},{160,128},{192,224},{224,1... | collective-permute-start | bytes 2359304 | tf_op jit(solution)/shard_map/panel_columns/ppermute | solution.py:22
  141.4 6.9 %copy-start.8 = (f32[4,128,384]{2,1,0:T(8,128)}, f32[4,128,384]{2,1,0:T(8,128)S(1)}, u32[]{:S(2)}) copy-start(f32[4,128,384]{2,1,0:T(8,128)S(1)} %collective-permute-done.25.refs_1_) | copy-start | bytes 2359300
  141.4 4.2 %collective-permute-start.27 = (f32[4,128,384]{2,1,0:T(8,128)S(1)}, f32[4,128,384]{2,1,0:T(8,128)}, u32[]{:S(2)}, u32[]{:S(2)}) collective-permute-start(f32[4,128,384]{2,1,0:T(8,128)S(1)} %collective-permute-done.25.refs_1_), channel_id=1, source_target_pairs={{0,32},{32,0},{64,96},{96,64},{128,160},{160,128},{192,224},{224,1... | collective-permute-start | bytes 2359304 | tf_op jit(solution)/shard_map/panel_columns/ppermute | solution.py:22
  143.7 9.3 %copy-start.26 = (s32[8]{0:T(128)}, s32[8]{0:T(128)S(1)}, u32[]{:S(2)}) copy-start(s32[8]{0:T(128)S(1)} %dynamic-slice_bitcast_fusion.tiles_ref) | copy-start | bytes 100
  143.8 4.4 %copy-start.9 = (f32[4,128,384]{2,1,0:T(8,128)}, f32[4,128,384]{2,1,0:T(8,128)S(1)}, u32[]{:S(2)}) copy-start(f32[4,128,384]{2,1,0:T(8,128)S(1)} %collective-permute-done.26.refs_2_) | copy-start | bytes 2359300
  154.0 16.1 %collective-permute-start.30 = (f32[384,128]{1,0:T(8,128)S(1)}, f32[384,128]{1,0:T(8,128)S(1)}, u32[]{:S(2)}, u32[]{:S(2)}) collective-permute-start(f32[384,128]{1,0:T(8,128)S(1)} %pad_maximum_fusion.5), channel_id=1, source_target_pairs={{0,1},{1,2},{2,3},{3,0},{4,5},{5,6},{6,7},{7,4},{8,9},{9,10},{10,1... | collective-permute-start | bytes 589832 | tf_op jit(solution)/shard_map/parent_rows/ppermute | solution.py:17
  155.9 11.7 %collective-permute-start.29 = (f32[384,128]{1,0:T(8,128)S(1)}, f32[384,128]{1,0:T(8,128)S(1)}, u32[]{:S(2)}, u32[]{:S(2)}) collective-permute-start(f32[384,128]{1,0:T(8,128)S(1)} %pad_maximum_fusion.5), channel_id=1, source_target_pairs={{0,3},{1,0},{2,1},{3,2},{4,7},{5,4},{6,5},{7,6},{8,11},{9,8},{10,9... | collective-permute-start | bytes 589832 | tf_op jit(solution)/shard_map/parent_rows/ppermute | solution.py:17
  167.7 10.0 %collective-permute-start.32 = (f32[384,128]{1,0:T(8,128)S(1)}, f32[384,128]{1,0:T(8,128)S(1)}, u32[]{:S(2)}, u32[]{:S(2)}) collective-permute-start(f32[384,128]{1,0:T(8,128)S(1)} %collective-permute-done.29), channel_id=1, source_target_pairs={{0,3},{1,0},{2,1},{3,2},{4,7},{5,4},{6,5},{7,6},{8,11},{9,8},{10,9... | collective-permute-start | bytes 589832 | tf_op jit(solution)/shard_map/parent_rows/ppermute | solution.py:17
  170.1 13.3 %copy-start.5 = (f32[512,128]{1,0:T(8,128)}, f32[512,128]{1,0:T(8,128)S(1)}, u32[]{:S(2)}) copy-start(f32[512,128]{1,0:T(8,128)S(1)} %pad_maximum_fusion.3.refs_2_) | copy-start | bytes 786436
  170.1 9.0 %collective-permute-start.31 = (f32[512,128]{1,0:T(8,128)S(1)}, f32[512,128]{1,0:T(8,128)S(1)}, u32[]{:S(2)}, u32[]{:S(2)}) collective-permute-start(f32[512,128]{1,0:T(8,128)S(1)} %pad_maximum_fusion.3.refs_2_), channel_id=1, source_target_pairs={{0,64},{32,96},{64,0},{96,32},{128,192},{160,224},{192,128},{224,1... | collective-permute-start | bytes 786440 | tf_op jit(solution)/shard_map/parent_rows/ppermute | solution.py:22
  172.2 6.9 %collective-permute-start.28 = (f32[256,128]{1,0:T(8,128)}, f32[256,128]{1,0:T(8,128)S(1)}, u32[]{:S(2)}, u32[]{:S(2)}) collective-permute-start(f32[256,128]{1,0:T(8,128)} %get-tuple-element.40.refs_0_), channel_id=1, source_target_pairs={{0,64},{32,96},{64,0},{96,32},{128,192},{160,224},{192,128},{224,1... | collective-permute-start | bytes 393224 | tf_op jit(solution)/shard_map/parent_rows/ppermute | solution.py:22
  177.7 5.7 %copy-start.7 = (f32[384,128]{1,0:T(8,128)}, f32[384,128]{1,0:T(8,128)S(1)}, u32[]{:S(2)}) copy-start(f32[384,128]{1,0:T(8,128)S(1)} %collective-permute-done.32.refs_4_) | copy-start | bytes 589828
  177.7 5.7 %collective-permute-start.33 = (f32[256,128]{1,0:T(8,128)S(1)}, f32[256,128]{1,0:T(8,128)S(1)}, u32[]{:S(2)}, u32[]{:S(2)}) collective-permute-start(f32[256,128]{1,0:T(8,128)S(1)} %slice.46), channel_id=1, source_target_pairs={{0,64},{32,96},{64,0},{96,32},{128,192},{160,224},{192,128},{224,1... | collective-permute-start | bytes 393224 | tf_op jit(solution)/shard_map/parent_rows/ppermute | solution.py:22
  179.1 4.3 %copy-start.23 = (f32[256,128]{1,0:T(8,128)}, f32[256,128]{1,0:T(8,128)S(1)}, u32[]{:S(2)}) copy-start(f32[256,128]{1,0:T(8,128)S(1)} %collective-permute-done.28.refs_1_) | copy-start | bytes 393220
  179.1 4.3 %copy-start.21 = (f32[512,128]{1,0:T(8,128)}, f32[512,128]{1,0:T(8,128)S(1)}, u32[]{:S(2)}) copy-start(f32[512,128]{1,0:T(8,128)S(1)} %collective-permute-done.31.refs_3_) | copy-start | bytes 786436
  187.4 3.3 %collective-permute-start.34 = (f32[256,128]{1,0:T(8,128)}, f32[256,128]{1,0:T(8,128)S(1)}, u32[]{:S(2)}, u32[]{:S(2)}) collective-permute-start(f32[256,128]{1,0:T(8,128)} %get-tuple-element.79), channel_id=1, source_target_pairs={{0,32},{32,0},{64,96},{96,64},{128,160},{160,128},{192,224},{224,1... | collective-permute-start | bytes 393224 | tf_op jit(solution)/shard_map/border_lower/ppermute | solution.py:22
  192.7 19.3 %all-to-all-start.2 = ((f32[8,256,128]{2,1,0:T(8,128)}), f32[8,256,128]{2,1,0:T(8,128)S(1)}, u32[]{:S(2)}, u32[]{:S(2)}) async-start(f32[8,256,128]{2,1,0:T(8,128)} %broadcast_in_dim.46), calls=%async_computation.2 | async-start | bytes 2097152 | tf_op jit(solution)/shard_map/border_lower/all_to_all | solution.py:160
  197.7 14.3 %copy-start.6 = (f32[4,128,128]{2,1,0:T(8,128)}, f32[4,128,128]{2,1,0:T(8,128)S(1)}, u32[]{:S(2)}) copy-start(f32[4,128,128]{2,1,0:T(8,128)S(1)} %pad_maximum_fusion.4.refs_0_) | copy-start | bytes 786436
  197.7 1.9 collective-permute-start.35
  199.6 12.4 %copy-start.22 = (f32[4,128,128]{2,1,0:T(8,128)}, f32[4,128,128]{2,1,0:T(8,128)S(1)}, u32[]{:S(2)}) copy-start(f32[4,128,128]{2,1,0:T(8,128)S(1)} %collective-permute-done.35.refs_1_) | copy-start | bytes 786436
  (3 other events, 2.4 us)
